TPU v7x, 32 devices: a whole 2x2x4 slice. The times are simulated.
32 devices in a mesh: gy: 4 (over z), gx: 8 (over y, x, core).
Axes of the slice: x: 2, y: 2, z: 4, core: 2. Of those that a mesh axis runs over, the one named last changes fastest.
Arguments:
- source_field: float32 [2, 1, 4096, 4096], P(None, None, 'gx', 'gy'), may hold values from -5 to 5
- receiver_field: float32 [2, 1, 4096, 4096], P(None, None, 'gx', 'gy'), may hold values from -5 to 5
- velocity_index: int32 [4, 4096, 4096], P(None, 'gx', 'gy'), may hold values from 0 to 63
- slowness: float32 [64], replicated, may hold values from 0.25 to 1
- freq_index: int32 [1], replicated, may hold values from 8 to 511
- root_modulus: float32 [1], replicated, may hold values from 0.9 to 1, as said below
- root_angle: float32 [1], replicated, may hold values from -3.140625 to 3.140625
Outputs:
- image: float32 [4, 4096, 4096], P(None, 'gx', 'gy')
- source_bottom: float32 [2, 1, 4096, 4096], P(None, None, 'gx', 'gy')
- receiver_top: float32 [2, 1, 4096, 4096], P(None, None, 'gx', 'gy')
Inputs may be any that keep to these rules, and one draw needn't show every extreme that they name: `root_modulus`: each modulus lies strictly below 1.
All inputs are finite; a program needn't handle non-finite values.
Results may differ from a plain program's by a relative error of at most 0.0003.
Values sent between devices are 32-bit elements; how exact they have to be, the bound alone decides.
No kernel may reach another device: no remote copies, remote signals or barrier semaphores. Data moves between devices by JAX's collectives and lax.ppermute only.
A program may use at most 192 MiB of HBM per device.

v0:
```python
import jax
import jax.numpy as jnp
from jax import lax
from jax.sharding import PartitionSpec as P

BLOCK = 128


HIGHEST = lax.Precision.HIGHEST
PHASE_UNIT = 0.05


def prefix(value, axis, join, neutral, backward):
    count, mine = (lax.axis_size(axis), lax.axis_index(axis))
    pieces = jax.tree.map(lambda part: lax.all_gather(part, axis), value)
    if backward:
        pieces = jax.tree.map(lambda part: part[::-1], pieces)
        mine = count - 1 - mine
    so_far = jax.tree.map(
        lambda part, zero: jnp.full_like(part, 0) + jnp.asarray(zero, part.dtype), value, neutral
    )

    def turn(position, so_far):
        longer = join(so_far, jax.tree.map(lambda part: part[position], pieces))
        return jax.tree.map(lambda new, old: jnp.where(position < mine, new, old), longer, so_far)

    return lax.fori_loop(0, count - 1, turn, so_far)


def powers(modulus, angle, exponent):
    radius_full = modulus.reshape((-1,) + (1,) * exponent.ndim)
    spin_full = angle.reshape((-1,) + (1,) * exponent.ndim)
    magnitude = jnp.exp(jnp.log(radius_full) * exponent)
    return (magnitude * jnp.cos(spin_full * exponent), magnitude * jnp.sin(spin_full * exponent))


def complex_mul(first_pair, second_pair):
    return (
        first_pair[0] * second_pair[0] - first_pair[1] * second_pair[1],
        first_pair[0] * second_pair[1] + first_pair[1] * second_pair[0],
    )


def complex_einsum(formula, left_pair, right_pair):
    real_part = jnp.einsum(formula, left_pair[0], right_pair[0], precision=HIGHEST) - jnp.einsum(
        formula, left_pair[1], right_pair[1], precision=HIGHEST
    )
    imag_part = jnp.einsum(formula, left_pair[0], right_pair[1], precision=HIGHEST) + jnp.einsum(
        formula, left_pair[1], right_pair[0], precision=HIGHEST
    )
    return (real_part, imag_part)


def combine_links(earlier, later):
    mult_pair = complex_mul((earlier[0], earlier[1]), (later[0], later[1]))
    value_pair = complex_mul((earlier[2], earlier[3]), (later[0], later[1]))
    return (mult_pair[0], mult_pair[1], value_pair[0] + later[2], value_pair[1] + later[3])


def link_start(carry_out, span_pow):
    return (
        jnp.ones_like(span_pow[0]),
        jnp.zeros_like(span_pow[1]),
        jnp.zeros_like(carry_out[0]),
        jnp.zeros_like(carry_out[1]),
    )


def x_link_ahead(carry_out, span_pow, modulus, angle, length):
    scanned = prefix(
        (span_pow[0], span_pow[1], carry_out[0], carry_out[1]),
        "gx",
        combine_links,
        link_start(carry_out, span_pow),
        False,
    )
    return (scanned[2], scanned[3])


def x_link_behind(carry_out, span_pow, modulus, angle, length):
    scanned = prefix(
        (span_pow[0], span_pow[1], carry_out[0], carry_out[1]),
        "gx",
        combine_links,
        link_start(carry_out, span_pow),
        True,
    )
    return (scanned[2], scanned[3])


def y_link_ahead(carry_out, span_pow, modulus, angle, length):
    scanned = prefix(
        (span_pow[0], span_pow[1], carry_out[0], carry_out[1]),
        "gy",
        combine_links,
        link_start(carry_out, span_pow),
        False,
    )
    return (scanned[2], scanned[3])


def y_link_behind(carry_out, span_pow, modulus, angle, length):
    scanned = prefix(
        (span_pow[0], span_pow[1], carry_out[0], carry_out[1]),
        "gy",
        combine_links,
        link_start(carry_out, span_pow),
        True,
    )
    return (scanned[2], scanned[3])


def line_pass(wave_field, modulus, angle, line_dim, backward, link_fn):
    channels = wave_field.shape[1]
    length = wave_field.shape[line_dim]
    width_blk = min(BLOCK, length)
    blocks = length // width_blk
    within = jnp.arange(width_blk, dtype=jnp.float32)
    block_pos = jnp.arange(blocks, dtype=jnp.float32)
    if backward:
        offset = within[None, :] - within[:, None]
        inner_steps = width_blk - 1.0 - within
        block_gap = block_pos[None, :] - block_pos[:, None]
        out_steps = block_pos
        entry_steps = blocks - 1.0 - block_pos
        edge_pos = 0
    else:
        offset = within[:, None] - within[None, :]
        inner_steps = within
        block_gap = block_pos[:, None] - block_pos[None, :]
        out_steps = blocks - 1.0 - block_pos
        entry_steps = block_pos
        edge_pos = width_blk - 1
    tail_re, tail_im = powers(modulus, angle, jnp.maximum(offset - 1.0, 0.0))
    weight = (1.0 - modulus * modulus)[:, None, None]
    root_re = modulus * jnp.cos(angle)
    root_im = modulus * jnp.sin(angle)
    strict = offset > 0.0
    on_diag = offset == 0.0
    mat_re = jnp.where(strict, weight * tail_re, jnp.where(on_diag, -root_re[:, None, None], 0.0))
    mat_im = jnp.where(strict, weight * tail_im, jnp.where(on_diag, root_im[:, None, None], 0.0))
    if line_dim == 2:
        shaped = wave_field.reshape(2, channels, blocks, width_blk, wave_field.shape[3])
        local_re, local_im = complex_einsum(
            "cij,cbjw->cbiw", (mat_re, mat_im), (shaped[0], shaped[1])
        )
        end_out = (local_re[:, :, edge_pos, :], local_im[:, :, edge_pos, :])
        end_in = (shaped[0][:, :, edge_pos, :], shaped[1][:, :, edge_pos, :])
    else:
        shaped = wave_field.reshape(2, channels, wave_field.shape[2], blocks, width_blk)
        local_re, local_im = complex_einsum(
            "cij,cwbj->cwbi", (mat_re, mat_im), (shaped[0], shaped[1])
        )
        end_out = (local_re[:, :, :, edge_pos], local_im[:, :, :, edge_pos])
        end_in = (shaped[0][:, :, :, edge_pos], shaped[1][:, :, :, edge_pos])
    rotated_end = complex_mul((root_re[:, None, None], root_im[:, None, None]), end_out)
    carries = (rotated_end[0] + end_in[0], rotated_end[1] + end_in[1])
    chain_re, chain_im = powers(modulus, angle, width_blk * jnp.maximum(block_gap - 1.0, 0.0))
    chain_re = jnp.where(block_gap > 0.0, chain_re, 0.0)
    chain_im = jnp.where(block_gap > 0.0, chain_im, 0.0)
    if line_dim == 2:
        entry_local = complex_einsum("cba,caw->cbw", (chain_re, chain_im), carries)
    else:
        entry_local = complex_einsum("cba,cwa->cwb", (chain_re, chain_im), carries)
    out_pair = powers(modulus, angle, width_blk * out_steps)
    if line_dim == 2:
        device_out = complex_einsum("ca,caw->cw", out_pair, carries)
    else:
        device_out = complex_einsum("ca,cwa->cw", out_pair, carries)
    span_pow = powers(modulus, angle, jnp.full((1,), float(length), jnp.float32))
    device_in = link_fn(device_out, span_pow, modulus, angle, length)
    enter_pair = powers(modulus, angle, width_blk * entry_steps)
    if line_dim == 2:
        added_in = complex_mul(
            (enter_pair[0][:, :, None], enter_pair[1][:, :, None]),
            (device_in[0][:, None, :], device_in[1][:, None, :]),
        )
    else:
        added_in = complex_mul(
            (enter_pair[0][:, None, :], enter_pair[1][:, None, :]),
            (device_in[0][:, :, None], device_in[1][:, :, None]),
        )
    entry_local = (entry_local[0] + added_in[0], entry_local[1] + added_in[1])
    inner_pow = powers(modulus, angle, inner_steps)
    if line_dim == 2:
        spread = complex_mul(
            (inner_pow[0][:, None, :, None], inner_pow[1][:, None, :, None]),
            (entry_local[0][:, :, None, :], entry_local[1][:, :, None, :]),
        )
    else:
        spread = complex_mul(
            (inner_pow[0][:, None, None, :], inner_pow[1][:, None, None, :]),
            (entry_local[0][:, :, :, None], entry_local[1][:, :, :, None]),
        )
    result = jnp.stack([local_re + spread[0], local_im + spread[1]])
    return result.reshape(wave_field.shape)


def x_sweep(wave_field, modulus, angle):
    ahead_pass = line_pass(wave_field, modulus, angle, 2, False, x_link_ahead)
    return line_pass(ahead_pass, modulus, angle, 2, True, x_link_behind)


def y_sweep(wave_field, modulus, angle):
    ahead_pass = line_pass(wave_field, modulus, angle, 3, False, y_link_ahead)
    return line_pass(ahead_pass, modulus, angle, 3, True, y_link_behind)


def on_device(
    source_field, receiver_field, velocity_index, slowness, freq_index, root_modulus, root_angle
):
    source, receiver = (source_field, receiver_field)
    depth_count = velocity_index.shape[0]
    channels = freq_index.shape[0]
    entry_ids = jnp.arange(slowness.shape[0], dtype=jnp.int32)
    phase_rate = freq_index.astype(jnp.float32)[:, None, None] * PHASE_UNIT
    levels = []
    for level_index in range(depth_count):
        matched = velocity_index[level_index][:, :, None] == entry_ids
        slow_cell = jnp.sum(jnp.where(matched, slowness, 0.0), axis=2)
        phase_arg = phase_rate * slow_cell[None]
        levels.append((jnp.cos(phase_arg), jnp.sin(phase_arg)))
    back_angle = -root_angle
    both_modulus = jnp.concatenate([root_modulus, root_modulus])
    both_angle = jnp.concatenate([root_angle, back_angle])
    source_levels = []
    receiver_levels = [None] * depth_count
    for depth_step in range(depth_count):
        source_levels.append(source)
        after_x = x_sweep(source, root_modulus, root_angle)
        cos_back, sin_back = levels[depth_count - 1 - depth_step]
        turned = jnp.stack(
            [
                receiver[0] * cos_back + receiver[1] * sin_back,
                receiver[1] * cos_back - receiver[0] * sin_back,
            ]
        )
        joined = y_sweep(jnp.concatenate([after_x, turned], axis=1), both_modulus, both_angle)
        cos_ahead, sin_ahead = levels[depth_step]
        ahead_part = joined[:, :channels]
        source = jnp.stack(
            [
                ahead_part[0] * cos_ahead - ahead_part[1] * sin_ahead,
                ahead_part[0] * sin_ahead + ahead_part[1] * cos_ahead,
            ]
        )
        receiver = x_sweep(joined[:, channels:], root_modulus, back_angle)
        receiver_levels[depth_count - 1 - depth_step] = receiver
    image_out = jnp.stack(
        [
            jnp.sum(source_now[0] * receiver_now[0] + source_now[1] * receiver_now[1], axis=0)
            for source_now, receiver_now in zip(source_levels, receiver_levels)
        ]
    )
    return (image_out, source, receiver)


def solution(mesh):
    placed = (
        P(None, None, "gx", "gy"),
        P(None, None, "gx", "gy"),
        P(None, "gx", "gy"),
        P(),
        P(),
        P(),
        P(),
    )
    return jax.shard_map(
        on_device,
        mesh=mesh,
        in_specs=placed,
        out_specs=(P(None, "gx", "gy"), P(None, None, "gx", "gy"), P(None, None, "gx", "gy")),
        check_vma=False,
    )
```

profile of v0, /device:TPU:0, one launch (start us, length us, event | category | flops | bytes accessed | tf_op | source)
XLA Modules:
  0.0 1797.5 jit_solution(6176490881907122258)
XLA Ops:
  8.1 128.8 %select_reduce_fusion = (f32[512,1024]{1,0:T(8,128)}, f32[512,1024]{1,0:T(8,128)}, f32[512,1024]{1,0:T(8,128)}, f32[512,1024]{1,0:T(8,128)S(1)}) fusion(s32[512,1024]{1,0:T(8,128)} %get-tuple-element.4604, f32[64]{0:T(128)S(1)} %copy-done.109, s32[512,1024]{1,0:T(8,128)} %get-tuple-element.4603, s32[512,1024]{1,0:T(8,128)} %get-tuple-element.4605, ...), kind=kLoop, calls=%fused_computation.208 | loop fusion | flops 400556032 | bytes 16777472 | tf_op jit(solution)/shard_map/reduce_sum | solution.py:220
  137.5 10.8 fusion.110
  164.6 15.1 all-reduce.4
  188.6 9.1 all-gather.3
  197.7 14.1 while.384
  235.6 9.1 all-gather.5
  244.7 14.7 while.385
  274.2 9.1 fusion.262
  314.1 11.1 all_gather.416
  333.3 13.1 all-gather.52
  346.8 13.1 all-gather.53
  409.8 13.1 all-gather.54
  423.3 13.1 all-gather.55
  482.7 9.1 all-gather.17
  491.7 12.5 while.390
  537.5 13.4 while.391
  561.7 18.0 %fusion.88 = (f32[1,1,512,1024]{3,2,1,0:T(8,128)}, f32[512,1024]{1,0:T(8,128)S(1)}, f32[512,1024]{1,0:T(8,128)S(1)}, f32[1,1,512,1024]{3,2,1,0:T(8,128)S(1)}, f3...) fusion(f32[512,1024]{1,0:T(8,128)} %get-tuple-element.4067, f32[]{:T(128)} %bitcast.72, ...), kind=kLoop, calls=%fused_computation.348 | loop fusion | flops 4194304 | bytes 25165828 | tf_op jit(solution)/shard_map/add | solution.py:234
  613.4 13.0 while.388
  650.5 9.1 all-gather.13
  659.5 13.9 while.389
  687.8 9.1 fusion.258
  731.9 13.1 all-gather.56
  745.4 13.1 all-gather.57
  814.2 13.1 all-gather.58
  827.7 13.1 all-gather.59
  902.4 14.1 while.396
  949.5 14.3 while.397
  972.8 11.7 fusion.35
  1020.1 13.4 while.394
  1066.7 14.2 while.395
  1095.1 9.1 fusion.254
  1139.3 13.1 all-gather.60
  1152.8 13.1 all-gather.61
  1221.6 13.1 all-gather.62
  1235.1 13.1 all-gather.63
  1319.0 13.6 while.402
  1365.6 13.8 while.403
  1422.6 13.4 while.400
  1459.9 9.1 all-gather.39
  1469.0 14.1 while.401
  1497.4 9.1 fusion.250
  1541.5 13.1 all-gather.64
  1555.0 13.1 all-gather.65
  1623.6 13.1 all-gather.66
  1637.1 13.1 all-gather.67
  1705.1 13.6 while.406
  1751.9 14.4 while.407
  1783.2 9.4 fusion.112
  (1132 shorter events, 1290.5 us)
Async XLA Ops:
  0.6 7.5 copy-start.109
  136.9 11.5 copy-start.42
  137.5 10.8 copy-start.68
  288.7 6.7 copy-start.61
  300.0 11.8 copy-start.43
  300.1 5.3 copy-start.1
  372.3 7.1 copy-start.45
  372.3 7.1 copy-start.60
  392.1 14.9 copy-start.47
  392.2 5.2 copy-start.8
  462.3 4.9 copy-start.32
  467.2 5.1 copy-start.76
  558.0 35.8 %copy-start.15 = (f32[1,1,512,1024]{3,2,1,0:T(8,128)}, f32[1,1,512,1024]{3,2,1,0:T(8,128)S(1)}, u32[]{:S(2)}) copy-start(f32[1,1,512,1024]{3,2,1,0:T(8,128)S(1)} %copy.707) | copy-start | bytes 6291460
  561.7 18.1 %copy-start.27 = (f32[1,4,128,1024]{3,2,1,0:T(8,128)S(1)}, f32[1,4,128,1024]{3,2,1,0:T(8,128)}, u32[]{:S(2)}) copy-start(f32[1,4,128,1024]{3,2,1,0:T(8,128)} %get-tuple-element.4698) | copy-start | bytes 6291460
  561.7 18.1 %copy-start.28 = (f32[1,4,128,1024]{3,2,1,0:T(8,128)S(1)}, f32[1,4,128,1024]{3,2,1,0:T(8,128)}, u32[]{:S(2)}) copy-start(f32[1,4,128,1024]{3,2,1,0:T(8,128)} %get-tuple-element.4699) | copy-start | bytes 6291460
  579.7 14.1 copy-start.23
  579.7 14.1 copy-start.25
  588.7 5.1 copy-start.92
  702.2 7.0 copy-start.62
  713.8 15.5 copy-start.54
  785.5 7.1 copy-start.65
  797.2 14.4 copy-start.51
  797.2 5.0 copy-start.10
  873.0 4.9 copy-start.35
  877.9 5.1 copy-start.93
  925.1 5.1 copy-start.83
  972.7 11.7 copy-start.29
  972.8 11.7 copy-start.38
  972.8 11.8 copy-start.39
  995.6 4.9 copy-start.84
  1109.6 7.0 copy-start.63
  1121.2 15.5 copy-start.55
  1192.8 7.1 copy-start.66
  1204.5 14.4 copy-start.52
  1204.5 5.0 copy-start.11
  1289.6 4.9 copy-start.36
  1294.5 5.1 copy-start.94
  1341.1 5.1 copy-start.85
  1380.1 4.7 copy-start.26
  1398.0 5.2 copy-start.79
  1511.9 6.7 copy-start.64
  1523.2 15.7 copy-start.49
  1594.8 7.1 copy-start.67
  1606.5 14.5 copy-start.46
  1606.5 5.0 copy-start.9
  1675.7 4.9 copy-start.37
  1680.6 5.1 copy-start.82
  1727.4 5.1 copy-start.73
  (63 other events, 169.2 us)
where the time goes:
time: 1810 us; the launch traced here: 1800 us
  other arithmetic  541 us (30%)
  blocking collectives  519 us (29%)
  matrix products  421 us (23%)
  local copies, waits for them, and re-layouts  303 us (17%)
    all_gather x50, blocking collectives, prefix(): pieces = jax.tree.map(lambda part: lax.all_gather(part, axis), value)  504 us
    select_n x136, other arithmetic, turn(): jnp.where(position < mine, new, old)  146 us
    reduce_sum x1, other arithmetic, on_device(): slow_cell = jnp.sum(jnp.where(matched, slowness, 0.0), axis=2)  129 us
    dot_general x72, matrix products, complex_einsum(): jnp.einsum(formula, left_pair[1], right_pair[1], precision=HIGHEST)  114 us
    dot_general x72, matrix products, complex_einsum(): jnp.einsum(formula, left_pair[1], right_pair[0], precision=HIGHEST)  108 us
    dot_general x72, matrix products, complex_einsum(): jnp.einsum(formula, left_pair[0], right_pair[0], precision=HIGHEST)  106 us
    add x25, other arithmetic, line_pass(): result = jnp.stack([local_re + spread[0], local_im + spread[1]])  97 us
    dot_general x72, matrix products, complex_einsum(): jnp.einsum(formula, left_pair[0], right_pair[1], precision=HIGHEST)  93.8 us

commit v1 on v0

v1 whole, which is shorter than its diff:
```python
import functools

import jax
import jax.numpy as jnp
import numpy as np
from jax import lax
from jax.experimental import pallas as pl
from jax.experimental.pallas import tpu as pltpu
from jax.sharding import PartitionSpec as P

PHASE_UNIT = 0.05
W = 128
F32 = jnp.float32
BF16 = jnp.bfloat16
HIGHEST = lax.Precision.HIGHEST
VMEM_LIMIT = 48 * 1024 * 1024


def complex_mul(a, b):
    return (a[0] * b[0] - a[1] * b[1], a[0] * b[1] + a[1] * b[0])


def root_powers(modulus, angle, exponent):
    k = exponent.astype(F32)
    coarse = jnp.round(angle * 512.0)
    fine = angle - coarse * (1.0 / 512.0)
    steps = k * coarse
    turns = jnp.round(steps * np.float32(1.0 / 512.0 / (2.0 * np.pi)))
    spin = (steps * (1.0 / 512.0) - turns * 6.28125) - turns * np.float32(2.0 * np.pi - 6.28125)
    spin = spin + k * fine
    magnitude = jnp.exp(jnp.log(modulus) * k)
    return (magnitude * jnp.cos(spin), magnitude * jnp.sin(spin))


def sweep_factors(modulus, angle):
    sin, cos = jnp.sin(angle), jnp.cos(angle)
    gap = (1.0 - modulus) * (1.0 + modulus)
    re, im = modulus * cos, modulus * sin
    den_re, den_im = gap + 2.0 * im * im, -2.0 * re * im
    den_sq = den_re * den_re + den_im * den_im
    inv = (den_re / den_sq, -den_im / den_sq)
    diag = (re * re - im * im + gap * gap * inv[0], -2.0 * re * im + gap * gap * inv[1])
    root_inv = (re / (modulus * modulus), -im / (modulus * modulus))
    off = complex_mul((0.0 * im, 2.0 * gap * im), complex_mul(root_inv, inv))
    end = (-gap * gap * inv[0], -gap * gap * inv[1])
    return diag, off, end


def real_rows(pair):
    re, im = pair
    rows, n = re.shape
    nb = n // W
    first = jnp.stack([re.reshape(rows, nb, W), -im.reshape(rows, nb, W)], axis=2)
    second = jnp.stack([im.reshape(rows, nb, W), re.reshape(rows, nb, W)], axis=2)
    return jnp.stack([first, second], axis=1).reshape(2 * rows, 2 * n)


def spread_rows(pair):
    re, im = pair
    rows, n = re.shape
    nb = n // W
    first = jnp.stack([re.reshape(rows, nb, W), im.reshape(rows, nb, W)], axis=2)
    second = jnp.stack([-im.reshape(rows, nb, W), re.reshape(rows, nb, W)], axis=2)
    return jnp.stack([first, second], axis=1).reshape(2 * rows, 2 * n)


def pad_rows(x, rows):
    return jnp.pad(x, ((0, rows - x.shape[0]), (0, 0)))


def halves(x):
    hi = x.astype(BF16)
    return hi, (x - hi.astype(F32)).astype(BF16)


def rounded_halves(x):
    hi = lax.reduce_precision(x, exponent_bits=8, mantissa_bits=7)
    return hi.astype(BF16), (x - hi).astype(BF16)


def state_exponents(length):
    nb = length // W
    m = np.arange(length)
    rows, masks = [], []
    for b in range(nb):
        rows += [b * W - 1 - m, m - (b + 1) * W]
        masks += [m < b * W, m >= (b + 1) * W]
    rows += [length - 1 - m, m]
    masks += [m >= 0, m >= 0]
    return np.maximum(np.stack(rows), 0).astype(np.int32), np.stack(masks)


def state_matrix(modulus, angle, length):
    exps, masks = state_exponents(length)
    re, im = root_powers(modulus, angle, jnp.asarray(exps))
    masks = jnp.asarray(masks)
    return real_rows((jnp.where(masks, re, 0.0), jnp.where(masks, im, 0.0)))


def link_coefs(modulus, angle, off, end, count, mine, length):
    other = jnp.arange(count, dtype=jnp.int32)
    far = root_powers(modulus, angle, length * (2 * count - 2 - mine - other))
    near = root_powers(modulus, angle, length * jnp.maximum(jnp.abs(other - mine) - 1, 0))
    root = (modulus * jnp.cos(angle), modulus * jnp.sin(angle))
    tail = complex_mul(end, far)
    head = complex_mul(complex_mul(off, root), near)
    before = other < mine
    one = jnp.ones((count,), F32)
    zero = jnp.zeros((count,), F32)
    send_f = (jnp.where(before, tail[0], one), jnp.where(before, tail[1], zero))
    send_b = (jnp.where(before, head[0], zero), jnp.where(before, head[1], zero))
    recv_f = (jnp.where(before, near[0], zero), jnp.where(before, near[1], zero))
    after = other > mine
    recv_b = (jnp.where(after, one, tail[0]), jnp.where(after, zero, tail[1]))
    return jnp.stack([*send_f, *send_b, *recv_f, *recv_b], axis=1)


def split3(x, first):
    hi, lo = halves(x)
    return jnp.concatenate([hi, lo, hi] if first else [hi, hi, lo], axis=0)


def nt(a, b):
    return lax.dot_general(a, b, (((1,), (1,)), ((), ())), preferred_element_type=F32)


def tn(a, b):
    return lax.dot_general(a, b, (((0,), (0,)), ((), ())), preferred_element_type=F32)


def nn(a, b):
    return lax.dot_general(a, b, (((1,), (0,)), ((), ())), preferred_element_type=F32)


def lookup(table, index):
    chunks = table.shape[0]
    out = None
    for c in range(chunks):
        row = jnp.broadcast_to(table[c : c + 1, :], index.shape)
        here = jnp.clip(index - c * W, 0, W - 1) if chunks > 1 else index
        got = jnp.take_along_axis(row, here, axis=1, mode="promise_in_bounds")
        out = got if out is None else jnp.where(index >= c * W, got, out)
    return out


def weigh(coef, row, col, pair):
    cr, ci = coef[row, col], coef[row, col + 1]
    return (cr * pair[0] - ci * pair[1], cr * pair[1] + ci * pair[0])


def add_pair(a, b):
    return b if a is None else (a[0] + b[0], a[1] + b[1])


def gather_entries(coef, recv, count, chain):
    first = second = None
    for e in range(count):
        pair = (recv[e, 2 * chain : 2 * chain + 1, :], recv[e, 2 * chain + 1 : 2 * chain + 2, :])
        first = add_pair(first, weigh(coef, e, 4, pair))
        second = add_pair(second, weigh(coef, e, 6, pair))
    return first, second


def write_pieces(coef, pieces, count, chain, f_pair, b_pair):
    for e in range(count):
        out = add_pair(weigh(coef, e, 0, f_pair), weigh(coef, e, 2, b_pair))
        pieces[e, 2 * chain : 2 * chain + 1, :] = out[0]
        pieces[e, 2 * chain + 1 : 2 * chain + 2, :] = out[1]


def put_turned(t_hi, t_lo, chain, b, pair):
    for part in range(2):
        hi, lo = halves(pair[part])
        t_hi[chain, 0, b * W : (b + 1) * W, part * W : (part + 1) * W] = hi
        t_lo[chain, 0, b * W : (b + 1) * W, part * W : (part + 1) * W] = lo


def y_states(t_hi, t_lo, st3, st_hi, coef_y, y_state, y_pieces, nby, county):
    rows = st_hi.shape[0]
    for chain in range(2):
        acc = jnp.zeros((2 * rows, W), F32)
        low = jnp.zeros((rows, W), F32)
        for b in range(nby):
            lanes = slice(2 * W * b, 2 * W * (b + 1))
            acc = acc + nt(st3[:, lanes], t_hi[chain, 0, b * W : (b + 1) * W, :])
            low = low + nt(st_hi[:, lanes], t_lo[chain, 0, b * W : (b + 1) * W, :])
        total = acc[:rows] + acc[rows:] + low
        y_state[chain] = total
        d = 4 * nby
        write_pieces(
            coef_y, y_pieces, county, chain,
            (total[d : d + 1], total[d + 1 : d + 2]), (total[d + 2 : d + 3], total[d + 3 : d + 4]),
        )


def first_kernel(nby, county, src, rec, idx, table, st3, st_hi, coef_y, t_hi, t_lo, y_state, y_pieces):
    for b in range(nby):
        lanes = slice(b * W, (b + 1) * W)
        put_turned(t_hi, t_lo, 0, b, (src[0, 0, :, lanes], src[1, 0, :, lanes]))
        index = idx[0, :, lanes]
        cos, sin = lookup(table[0], index), lookup(table[1], index)
        put_turned(t_hi, t_lo, 1, b, complex_mul((rec[0, 0, :, lanes], -rec[1, 0, :, lanes]), (cos, sin)))
    y_states(t_hi, t_lo, st3, st_hi, coef_y, y_state, y_pieces, nby, county)


def local_kernel(nby, t_hi, t_lo, y_state, my_hi, my_lo, sp_y, lx_h, lx_l, w_out, x_state, vx_hi, vx_lo):
    a = pl.program_id(1)
    srows = lx_l.shape[1] - 2 * W
    main = nn(t_hi[0, 0], my_hi[...]) + nn(t_hi[0, 0], my_lo[...]) + nn(t_lo[0, 0], my_hi[...])
    for b in range(nby):
        st = split3(y_state[0, 4 * b : 4 * b + 4, :], True)
        v = main[b * W : (b + 1) * W] + tn(st, sp_y[...])
        hi, lo = halves(v)
        for part in range(2):
            vx_hi[part * W : (part + 1) * W, b * W : (b + 1) * W] = hi[:, part * W : (part + 1) * W]
            vx_lo[part * W : (part + 1) * W, b * W : (b + 1) * W] = lo[:, part * W : (part + 1) * W]
    high = nn(lx_h[0], vx_hi[...])
    low = nn(lx_l[0], vx_lo[...])
    w_out[0, 0] = high[: 2 * W] + high[2 * W : 4 * W] + low[: 2 * W]
    states = high[4 * W : 4 * W + srows] + high[4 * W + srows :] + low[2 * W :]

    @pl.when(a == 0)
    def _():
        x_state[0] = states

    @pl.when(a > 0)
    def _():
        x_state[0] += states


def link_kernel(
    nbx, county, countx, recv_y, x_local, coef_y, coef_x, sx, edge, mxt, x_state, ym, x_pieces
):
    for chain in range(2):
        (fr, fi), (br, bi) = gather_entries(coef_y, recv_y, county, chain)
        cols = []
        for a in range(nbx):
            lanes = slice(a * W, (a + 1) * W)
            top = jnp.concatenate([fr[:, lanes], fi[:, lanes]], axis=1)
            top2 = jnp.concatenate([-fi[:, lanes], fr[:, lanes]], axis=1)
            bot = jnp.concatenate([br[:, lanes], bi[:, lanes]], axis=1)
            bot2 = jnp.concatenate([-bi[:, lanes], br[:, lanes]], axis=1)
            cols.append(jnp.concatenate([top, top2, bot, bot2, jnp.zeros((4, 2 * W), F32)], axis=0))
        gain = None
        for a in range(nbx):
            ym[chain, :, 2 * W * a : 2 * W * (a + 1)] = lax.dot_general(
                cols[a], mxt[...], (((1,), (0,)), ((), ())), precision=HIGHEST, preferred_element_type=F32
            )
            part = lax.dot_general(
                sx[:, 2 * W * a : 2 * W * (a + 1)], cols[a], (((1,), (1,)), ((), ())),
                precision=HIGHEST, preferred_element_type=F32,
            )
            gain = part if gain is None else gain + part
        total = x_local[chain]
        for s in range(4):
            total = total + gain[:, s : s + 1] * edge[s : s + 1, :]
        for a in range(nbx):
            x_state[chain, a, 0:4, :] = total[4 * a : 4 * a + 4, :]
            x_state[chain, a, 4:8, :] = jnp.zeros((4, total.shape[1]), F32)
        d = 4 * nbx
        write_pieces(
            coef_x, x_pieces, countx, chain,
            (total[d : d + 1], total[d + 1 : d + 2]), (total[d + 2 : d + 3], total[d + 3 : d + 4]),
        )


def post_kernel(plan, nby, county, countx, *refs):
    refs = list(refs)
    take = lambda: refs.pop(0)
    w_in, x_state, ym, recv_x, coef_x, edge, sp_x, sp_dev, table = (take() for _ in range(9))
    idx_s = take()
    idx_r = take() if plan["turn"] else None
    st3, st_hi, coef_y = (take(), take(), take()) if plan["turn"] else (None,) * 3
    olds = [{"s": (take(), take()) if z[1] == "split" else take() if z[1] == "field" else None,
             "r": take() if z[2] else None} for z in plan["images"]]
    if plan["turn"]:
        t_hi, t_lo, y_state, y_pieces = (take() for _ in range(4))
    else:
        src_out, rec_out = take(), take()
    keep_out = take() if plan["keep"] else None
    image_outs = [take() for _ in plan["images"]]

    lefts, rights = [], []
    for chain in range(2):
        first, second = gather_entries(coef_x, recv_x, countx, chain)
        mine = x_state[chain, 0, 0:4, :]
        right = jnp.concatenate([mine, *first, *second, edge[0:4, :]], axis=0)
        left = jnp.concatenate([sp_x[...], sp_dev[0], ym[chain, 0:4, :]], axis=0)
        rights.append(split3(right, False))
        lefts.append(split3(left, True))
    for b in range(nby):
        lanes = slice(b * W, (b + 1) * W)
        fields = []
        for chain in range(2):
            u = w_in[chain, 0, :, lanes] + tn(lefts[chain], rights[chain][:, lanes])
            fields.append((u[:W], u[W:]))
        index = idx_s[0, :, lanes]
        source = complex_mul(fields[0], (lookup(table[0], index), lookup(table[1], index)))
        back = fields[1]
        if plan["turn"]:
            put_turned(t_hi, t_lo, 0, b, source)
            index = idx_r[0, :, lanes]
            put_turned(t_hi, t_lo, 1, b, complex_mul(back, (lookup(table[0], index), lookup(table[1], index))))
        else:
            src_out[0, 0, :, lanes], src_out[1, 0, :, lanes] = source
            rec_out[0, 0, :, lanes], rec_out[1, 0, :, lanes] = back[0], -back[1]
        if keep_out is not None:
            keep_out[0, :, lanes], keep_out[1, :, lanes] = back
        for old, (_, how, has_r), out in zip(olds, plan["images"], image_outs):
            if how == "split":
                hi, lo = old["s"]
                rows = slice(b * W, (b + 1) * W)
                s = [hi[0, 0, rows, p * W : (p + 1) * W].astype(F32) + lo[0, 0, rows, p * W : (p + 1) * W].astype(F32)
                     for p in range(2)]
            elif how == "field":
                s = (old["s"][0, 0, :, lanes], old["s"][1, 0, :, lanes])
            else:
                s = source
            r = (old["r"][0, :, lanes], old["r"][1, :, lanes]) if has_r else back
            out[:, lanes] = s[0] * r[0] - s[1] * r[1]
    if plan["turn"]:
        y_states(t_hi, t_lo, st3, st_hi, coef_y, y_state, y_pieces, nby, county)


def whole(shape):
    return pl.BlockSpec(shape, lambda *_: (0,) * len(shape))


SMEM = pl.BlockSpec(memory_space=pltpu.SMEM)


def params(dims):
    return pltpu.CompilerParams(vmem_limit_bytes=VMEM_LIMIT, dimension_semantics=("arbitrary",) * dims)


def on_device(source_field, receiver_field, velocity_index, slowness, freq_index, root_modulus, root_angle):
    depth, len_x, len_y = velocity_index.shape
    nbx, nby = len_x // W, len_y // W
    countx, county = lax.axis_size("gx"), lax.axis_size("gy")
    modulus, angle = root_modulus[0], root_angle[0]
    diag, off, end = sweep_factors(modulus, angle)

    entries = slowness.shape[0]
    chunks = -(-entries // W)
    rate = freq_index.astype(F32)[0] * PHASE_UNIT
    phase = jnp.pad(rate * slowness, (0, chunks * W - entries)).reshape(chunks, W)
    table = jnp.stack([jnp.cos(phase), jnp.sin(phase)])

    at = np.arange(W)
    dist = np.abs(at[:, None] - at[None, :]).astype(np.int32)
    pw = root_powers(modulus, angle, jnp.asarray(dist))
    pw = complex_mul(off, pw)
    on = jnp.asarray(dist == 0)
    mr, mi = jnp.where(on, diag[0], pw[0]), jnp.where(on, diag[1], pw[1])
    my = jnp.concatenate([jnp.concatenate([mr, mi], 1), jnp.concatenate([-mi, mr], 1)], 0)
    mx = jnp.concatenate([jnp.concatenate([mr, -mi], 1), jnp.concatenate([mi, mr], 1)], 0)
    my_hi, my_lo = rounded_halves(my)
    mx_hi, mx_lo = rounded_halves(mx)

    rows_y = -(-(4 * nby + 4) // 16) * 16
    rows_x = -(-(4 * nbx + 4) // 16) * 16
    st_hi, st_lo = rounded_halves(pad_rows(state_matrix(modulus, angle, len_y), rows_y))
    st3 = jnp.concatenate([st_hi, st_lo], axis=0)
    sx = pad_rows(state_matrix(modulus, angle, len_x), rows_x)
    sx_hi, sx_lo = rounded_halves(sx)
    blocks_of = lambda x: x.reshape(rows_x, nbx, 2 * W).transpose(1, 0, 2)
    rep = lambda x: jnp.broadcast_to(x[None], (nbx,) + x.shape)
    lx_h = jnp.concatenate([rep(mx_hi), rep(mx_lo), blocks_of(sx_hi), blocks_of(sx_lo)], axis=1)
    lx_l = jnp.concatenate([rep(mx_hi), blocks_of(sx_hi)], axis=1)

    near = complex_mul(off, root_powers(modulus, angle, jnp.asarray(np.stack([at + 1, W - at]).astype(np.int32))))
    spread = spread_rows(near)
    sp_hi, sp_lo = rounded_halves(spread)
    sp_y = jnp.concatenate([sp_hi, sp_hi, sp_lo], axis=0)

    def edges(length):
        m = np.arange(length)
        ahead = complex_mul(off, root_powers(modulus, angle, jnp.asarray((m + 1).astype(np.int32))))
        behind = root_powers(modulus, angle, jnp.asarray((length - 1 - m).astype(np.int32)))
        return jnp.stack([ahead[0], behind[0]]), jnp.stack([ahead[1], behind[1]])

    edge_x = spread_rows(edges(len_x)).reshape(4, nbx, 2 * W).transpose(1, 0, 2)
    er, ei = edges(len_y)
    edge_y = jnp.concatenate([jnp.stack([er, ei], axis=1).reshape(4, len_y), jnp.zeros((4, len_y), F32)], axis=0)

    coef_y = link_coefs(modulus, angle, off, end, county, lax.axis_index("gy"), len_y)
    coef_x = link_coefs(modulus, angle, off, end, countx, lax.axis_index("gx"), len_x)

    turned = jax.ShapeDtypeStruct((2, nbx, nby * W, 2 * W), BF16)
    turned_spec = pl.BlockSpec((2, 1, nby * W, 2 * W), lambda a: (0, a, 0, 0))
    y_state_shape = jax.ShapeDtypeStruct((2, rows_y, len_x), F32)
    y_state_spec = pl.BlockSpec((2, rows_y, W), lambda a: (0, 0, a))
    y_piece_shape = jax.ShapeDtypeStruct((county, 4, len_x), F32)
    y_piece_spec = pl.BlockSpec((county, 4, W), lambda a: (0, 0, a))
    field_spec = pl.BlockSpec((2, 1, W, len_y), lambda a: (0, 0, a, 0))
    keep_spec = pl.BlockSpec((2, W, len_y), lambda a: (0, a, 0))
    image_spec = pl.BlockSpec((W, len_y), lambda a: (a, 0))
    level_spec = lambda z: pl.BlockSpec((1, W, len_y), lambda a: (z, a, 0))
    turn_out = [turned, turned, y_state_shape, y_piece_shape]
    turn_specs = [turned_spec, turned_spec, y_state_spec, y_piece_spec]

    t_hi, t_lo, y_state, y_pieces = pl.pallas_call(
        functools.partial(first_kernel, nby, county),
        grid=(nbx,),
        in_specs=[field_spec, field_spec, level_spec(depth - 1), whole(table.shape), whole(st3.shape),
                  whole(st_hi.shape), SMEM],
        out_specs=turn_specs,
        out_shape=turn_out,
        compiler_params=params(1),
        name="first",
    )(source_field, receiver_field, velocity_index, table, st3, st_hi, coef_y)

    local = pl.pallas_call(
        functools.partial(local_kernel, nby),
        grid=(2, nbx),
        in_specs=[
            pl.BlockSpec((1, 1, nby * W, 2 * W), lambda c, a: (c, a, 0, 0)),
            pl.BlockSpec((1, 1, nby * W, 2 * W), lambda c, a: (c, a, 0, 0)),
            pl.BlockSpec((1, rows_y, W), lambda c, a: (c, 0, a)),
            whole(my_hi.shape), whole(my_lo.shape), whole(sp_y.shape),
            pl.BlockSpec((1,) + lx_h.shape[1:], lambda c, a: (a, 0, 0)),
            pl.BlockSpec((1,) + lx_l.shape[1:], lambda c, a: (a, 0, 0)),
        ],
        out_specs=[
            pl.BlockSpec((1, 1, 2 * W, len_y), lambda c, a: (c, a, 0, 0)),
            pl.BlockSpec((1, rows_x, len_y), lambda c, a: (c, 0, 0)),
        ],
        out_shape=[
            jax.ShapeDtypeStruct((2, nbx, 2 * W, len_y), F32),
            jax.ShapeDtypeStruct((2, rows_x, len_y), F32),
        ],
        scratch_shapes=[pltpu.VMEM((2 * W, len_y), BF16)] * 2,
        compiler_params=params(2),
        name="local",
    )

    link = pl.pallas_call(
        functools.partial(link_kernel, nbx, county, countx),
        in_specs=[pl.BlockSpec(memory_space=pltpu.VMEM)] * 2 + [SMEM] * 2 + [pl.BlockSpec(memory_space=pltpu.VMEM)] * 3,
        out_shape=[
            jax.ShapeDtypeStruct((2, nbx, 8, len_y), F32),
            jax.ShapeDtypeStruct((2, 8, 2 * len_x), F32),
            jax.ShapeDtypeStruct((countx, 4, len_y), F32),
        ],
        compiler_params=params(0),
        name="link",
    )

    source_levels = {0: ("field", (source_field,))}
    kept = {}
    images = [None] * depth
    for step in range(depth):
        w, x_local = local(t_hi, t_lo, y_state, my_hi, my_lo, sp_y, lx_h, lx_l)
        recv_y = lax.all_to_all(y_pieces, "gy", 0, 0)
        x_state, ym, x_pieces = link(recv_y, x_local, coef_y, coef_x, sx, edge_y, mx.T)
        recv_x = lax.all_to_all(x_pieces, "gx", 0, 0)
        turn = step < depth - 1
        level_r = depth - 1 - step
        todo = [z for z in range(depth) if max(z - 1, depth - 1 - z) == step]
        plan = {
            "turn": turn,
            "keep": level_r - 1 > step,
            "images": [(z, None if z - 1 == step else source_levels[z][0], z != level_r) for z in todo],
        }
        args = [w, x_state, ym, recv_x, coef_x, edge_y, spread, edge_x, table, velocity_index]
        specs = [
            pl.BlockSpec((2, 1, 2 * W, len_y), lambda a: (0, a, 0, 0)),
            pl.BlockSpec((2, 1, 8, len_y), lambda a: (0, a, 0, 0)),
            pl.BlockSpec((2, 8, 2 * W), lambda a: (0, 0, a)),
            whole(recv_x.shape), SMEM, whole(edge_y.shape), whole(spread.shape),
            pl.BlockSpec((1, 4, 2 * W), lambda a: (a, 0, 0)),
            whole(table.shape), level_spec(step),
        ]
        if turn:
            args += [velocity_index, st3, st_hi, coef_y]
            specs += [level_spec(depth - 2 - step), whole(st3.shape), whole(st_hi.shape), SMEM]
        for z, how, has_r in plan["images"]:
            if how == "split":
                args += source_levels[z][1]
                specs += [pl.BlockSpec((1, 1, nby * W, 2 * W), lambda a: (0, a, 0, 0))] * 2
            elif how == "field":
                args += source_levels[z][1]
                specs += [field_spec]
            if has_r:
                args += [kept[z]]
                specs += [keep_spec]
        if turn:
            shapes, out_specs = list(turn_out), list(turn_specs)
        else:
            shapes = [jax.ShapeDtypeStruct(source_field.shape, F32)] * 2
            out_specs = [field_spec] * 2
        if plan["keep"]:
            shapes.append(jax.ShapeDtypeStruct((2, len_x, len_y), F32))
            out_specs.append(keep_spec)
        shapes += [jax.ShapeDtypeStruct((len_x, len_y), F32)] * len(todo)
        out_specs += [image_spec] * len(todo)
        outs = pl.pallas_call(
            functools.partial(post_kernel, plan, nby, county, countx),
            grid=(nbx,),
            in_specs=specs,
            out_specs=out_specs,
            out_shape=shapes,
            compiler_params=params(1),
            name="post",
        )(*args)
        outs = list(outs)
        if turn:
            t_hi, t_lo, y_state, y_pieces = outs[:4]
            outs = outs[4:]
            source_levels[step + 1] = ("split", (t_hi, t_lo))
        else:
            source, receiver = outs[:2]
            outs = outs[2:]
        if plan["keep"]:
            kept[level_r] = outs.pop(0)
        for z in todo:
            images[z] = outs.pop(0)
    return jnp.stack(images), source, receiver


def solution(mesh):
    placed = (
        P(None, None, "gx", "gy"),
        P(None, None, "gx", "gy"),
        P(None, "gx", "gy"),
        P(),
        P(),
        P(),
        P(),
    )
    return jax.shard_map(
        on_device,
        mesh=mesh,
        in_specs=placed,
        out_specs=(P(None, "gx", "gy"), P(None, None, "gx", "gy"), P(None, None, "gx", "gy")),
        check_vma=False,
    )
```

time: 1810 us -> 230 us (0.13)
  other arithmetic: 541 us -> 10 us
  blocking collectives: 519 us -> 23.8 us
  matrix products: 421 us -> 0 us
  local copies, waits for them, and re-layouts: 303 us -> 18.4 us
  Pallas kernels: 0 us -> 144 us
  starting transfers between devices: 0 us -> 25.3 us
    all_gather x50 -> x0, blocking collectives: 504 us -> none  [prefix(): pieces = jax.tree.map(lambda part: lax.all_gather(part, axis), value)]
    dot_general x288 -> x0, matrix products: 421 us -> none  [the longest x72 114 us: complex_einsum(): jnp.einsum(formula, left_pair[1], right_pair[1], precision=HIGHEST)]
    add x81 -> x0, other arithmetic: 196 us -> none  [the longest x25 97 us: line_pass(): result = jnp.stack([local_re + spread[0], local_im + spread[1]])]
    pallas_call x0 -> x13, Pallas kernels: none -> 144 us  [the longest x4 77.1 us: on_device(): w, x_local = local(t_hi, t_lo, y_state, my_hi, my_lo, sp_y, lx_h, lx_l)]
    select_n x136 -> x10, other arithmetic: 146 us -> 1.95 us  [the longest x2 1.48 us: state_matrix(): return real_rows((jnp.where(masks, re, 0.0), jnp.where(masks, im, 0.0)))]
    reduce_sum x1 -> x0, other arithmetic: 129 us -> none  [on_device(): slow_cell = jnp.sum(jnp.where(matched, slowness, 0.0), axis=2)]
    slice x39 -> x0, local copies, waits for them, and re-layouts: 102 us -> none  [the longest x12 46.3 us: line_pass(): shaped[0]]
    dynamic_slice x112 -> x0, local copies, waits for them, and re-layouts: 71.8 us -> none  [turn(): longer = join(so_far, jax.tree.map(lambda part: part[position], pieces))]
  transfers between devices with their start and end apart: 0 -> 5, of which waited for: 0 -> 1; matrix products, arithmetic and copies ran while one was open for 0% -> 2% of each run, Pallas kernels for 0% -> 34%
where the time goes in v1:
time: 230 us; the launch traced here: 229 us
  Pallas kernels  144 us (63%)
  starting transfers between devices  25.3 us (11%)
  blocking collectives  23.8 us (10%)
  local copies, waits for them, and re-layouts  18.4 us (8%)
  other arithmetic  10 us (4%)
  waiting for transfers between devices  4.03 us (2%)
  between operations  3.54 us (2%)
    pallas_call x4, Pallas kernels, on_device(): w, x_local = local(t_hi, t_lo, y_state, my_hi, my_lo, sp_y, lx_h, lx_l)  77.1 us
    pallas_call x4, Pallas kernels, on_device(): pl.pallas_call(functools.partial(post_kernel, plan, nby, county, countx),...  49.8 us
    all_to_all x3, blocking collectives, on_device(): recv_x = lax.all_to_all(x_pieces, 'gx', 0, 0)  23.8 us
    all_to_all x4, starting transfers between devices, on_device(): recv_y = lax.all_to_all(y_pieces, 'gy', 0, 0)  21.6 us
    unnamed x65, local copies, waits for them, and re-layouts  17.1 us
    pallas_call x4, Pallas kernels, on_device(): link(recv_y, x_local, coef_y, coef_x, sx, edge_y, mx.T)  9.11 us
    pallas_call x1, Pallas kernels, on_device(): pl.pallas_call(functools.partial(first_kernel, nby, county), grid=(nbx,),...  8.31 us
  transfers between devices with their start and end apart: 5, of which 1 were waited for; matrix products, arithmetic and copies ran while one was open for 2% of the time, Pallas kernels for 34%

profile of v1, /device:TPU:0, one launch (start us, length us, event | category | flops | bytes accessed | tf_op | source)
XLA Modules:
  0.0 229.4 jit_solution(7182643007832924243)
XLA Ops:
  3.2 0.7 broadcast_multiply_fusion
  3.9 1.3 multiply_select_fusion
  5.5 0.2 maximum_bitcast_fusion
  6.5 8.3 %first.1 = (bf16[2,4,1024,256]{3,2,1,0:T(8,128)(2,1)S(1)}, bf16[2,4,1024,256]{3,2,1,0:T(8,128)(2,1)}, f32[2,48,512]{2,1,0:T(8,128)S(1)}, f32[4,4,512]{2,1,0:T(4,128)}) custom-call(f32[2,1,512,1024]{3,2,1,0:T(8,128)} %refs_10_.7, f32[2,1,512,1024]{3,2,1,0:T(8,128)} %rec.1, s32[4,512,1024]{2,1,0:T(8,128)} %refs_9_.7, ...), custom_call_target="tpu_custom_call" | custom-call | tf_op jit(solution)/shard_map/first/pallas_call | solution.py:402
  14.8 2.0 copy-done.1
  16.8 6.3 %all-to-all-start = ((f32[4,4,512]{2,1,0:T(4,128)}), f32[4,4,512]{2,1,0:T(4,128)S(1)}, u32[]{:S(2)}, u32[]{:S(2)}) async-start(f32[4,4,512]{2,1,0:T(4,128)} %get-tuple-element.50), calls=%async_computation | async-start | bytes 65536 | tf_op jit(solution)/shard_map/all_to_all | solution.py:454
  23.4 0.3 fusion.67
  24.1 0.4 copy-done.21
  25.2 0.7 sine_multiply_fusion.5
  26.1 0.3 copy-done.23
  26.5 0.6 maximum_negate_fusion
  27.4 19.3 %local.4 = (f32[2,4,256,1024]{3,2,1,0:T(8,128)}, f32[2,32,1024]{2,1,0:T(8,128)S(1)}) custom-call(bf16[2,4,1024,256]{3,2,1,0:T(8,128)(2,1)} %copy-done.1, bf16[2,4,1024,256]{3,2,1,0:T(8,128)(2,1)} %get-tuple-element.47.t_lo, f32[2,48,512]{2,1,0:T(8,128)S(1)} %get-tuple-element.48.y_state, bf16[256,256]{1,0:T(8,128)(2,1)S(1)} %copy.29.my_hi, ...), custom_call_target="tpu_custom_call" | custom-call | tf_op jit(solution)/shard_map/local/pallas_call | solution.py:453
  46.7 0.7 copy-done.8
  47.4 0.9 copy-done.9
  48.3 2.3 link.4
  50.6 0.6 copy-done.14
  51.3 3.7 %all-to-all-start.1 = ((f32[8,4,1024]{2,1,0:T(4,128)}), f32[8,4,1024]{2,1,0:T(4,128)S(1)}, u32[]{:S(2)}, u32[]{:S(2)}) async-start(f32[8,4,1024]{2,1,0:T(4,128)} %copy-done.14), calls=%async_computation.1 | async-start | bytes 262144 | tf_op jit(solution)/shard_map/all_to_all | solution.py:456
  55.0 0.8 maximum_bitcast_fusion.4
  55.8 0.7 copy.48
  56.5 4.0 %all-to-all-done.1.refs_3_ = f32[8,4,1024]{2,1,0:T(4,128)S(1)} async-done(((f32[8,4,1024]{2,1,0:T(4,128)}), f32[8,4,1024]{2,1,0:T(4,128)S(1)}, u32[]{:S(2)}, u32[]{:S(2)}) %all-to-all-start.1) | async-done | bytes 131104 | tf_op jit(solution)/shard_map/all_to_all | solution.py:456
  60.5 0.8 copy-done.16
  61.4 0.7 copy-done.18
  62.0 12.1 %post.4 = (bf16[2,4,1024,256]{3,2,1,0:T(8,128)(2,1)S(1)}, bf16[2,4,1024,256]{3,2,1,0:T(8,128)(2,1)}, f32[2,48,512]{2,1,0:T(8,128)S(1)}, f32[4,4,512]{2,1,0:T(4,128)S(1)}, f32[2,512,1024]{2,1,0:T(8,128)}) custom-call(f32[2,4,256,1024]{3,2,1,0:T(8,128)} %get-tuple-element.49.refs_0_, f32[2,4,8,1024]{3,2,1,0:T(8,128)S(1)} %get-tuple-element.52.refs_1_, ...), custom_call_target="tpu_custom_call" | custom-call | tf_op jit(solution)/shard_map/post/pallas_call | solution.py:497
  74.2 2.0 copy-done
  76.2 0.7 copy-done.10
  76.8 0.6 copy-done.19
  77.5 5.1 %all-to-all-start.2 = ((f32[4,4,512]{2,1,0:T(4,128)}), f32[4,4,512]{2,1,0:T(4,128)S(1)}, u32[]{:S(2)}, u32[]{:S(2)}) async-start(f32[4,4,512]{2,1,0:T(4,128)} %copy-done.19), calls=%async_computation.2 | async-start | bytes 65536 | tf_op jit(solution)/shard_map/all_to_all | solution.py:454
  82.5 0.9 copy-done.11
  83.5 19.3 %local.5 = (f32[2,4,256,1024]{3,2,1,0:T(8,128)}, f32[2,32,1024]{2,1,0:T(8,128)S(1)}) custom-call(bf16[2,4,1024,256]{3,2,1,0:T(8,128)(2,1)} %copy-done, bf16[2,4,1024,256]{3,2,1,0:T(8,128)(2,1)} %get-tuple-element.56.t_lo.refs_15_, f32[2,48,512]{2,1,0:T(8,128)S(1)} %copy-done.11, bf16[256,256]{1,0:T(8,128)(2,1)S(1)} %copy.29.my_hi, ...), custom_call_target="tpu_custom_call" | custom-call | tf_op jit(solution)/shard_map/local/pallas_call | solution.py:453
  102.7 2.3 link.5
  105.0 7.9 %all_to_all.40.refs_3_ = f32[8,4,1024]{2,1,0:T(4,128)S(1)} all-to-all(f32[8,4,1024]{2,1,0:T(4,128)S(1)} %get-tuple-element.63), channel_id=1, replica_groups=mesh['gy'=4,'gx'=8] {'gx'}, dimensions={0} | all-to-all | bytes 262144 | tf_op jit(solution)/shard_map/all_to_all | solution.py:456
  112.9 12.7 %post.5 = (bf16[2,4,1024,256]{3,2,1,0:T(8,128)(2,1)}, bf16[2,4,1024,256]{3,2,1,0:T(8,128)(2,1)}, f32[2,48,512]{2,1,0:T(8,128)S(1)}, f32[4,4,512]{2,1,0:T(4,128)}, f32[512,1024]{1,0:T(8,128)S(1)}) custom-call(f32[2,4,256,1024]{3,2,1,0:T(8,128)} %get-tuple-element.58.refs_0_, f32[2,4,8,1024]{3,2,1,0:T(8,128)S(1)} %get-tuple-element.61.refs_1_, ...), custom_call_target="tpu_custom_call" | custom-call | tf_op jit(solution)/shard_map/post/pallas_call | solution.py:497
  125.7 1.3 copy-done.2
  127.0 0.7 copy-done.12
  127.7 5.1 %all-to-all-start.4 = ((f32[4,4,512]{2,1,0:T(4,128)}), f32[4,4,512]{2,1,0:T(4,128)S(1)}, u32[]{:S(2)}, u32[]{:S(2)}) async-start(f32[4,4,512]{2,1,0:T(4,128)} %get-tuple-element.68), calls=%async_computation.4 | async-start | bytes 65536 | tf_op jit(solution)/shard_map/all_to_all | solution.py:454
  132.8 0.9 copy-done.13
  133.7 19.3 %local.6 = (f32[2,4,256,1024]{3,2,1,0:T(8,128)}, f32[2,32,1024]{2,1,0:T(8,128)S(1)}) custom-call(bf16[2,4,1024,256]{3,2,1,0:T(8,128)(2,1)} %get-tuple-element.64.t_hi, bf16[2,4,1024,256]{3,2,1,0:T(8,128)(2,1)} %get-tuple-element.65.t_lo, f32[2,48,512]{2,1,0:T(8,128)S(1)} %copy-done.13, bf16[256,256]{1,0:T(8,128)(2,1)S(1)} %copy.29.my_hi, ...), custom_call_target="tpu_custom_call" | custom-call | tf_op jit(solution)/shard_map/local/pallas_call | solution.py:453
  153.0 2.3 link.6
  155.2 7.9 %all_to_all.41.refs_3_ = f32[8,4,1024]{2,1,0:T(4,128)S(1)} all-to-all(f32[8,4,1024]{2,1,0:T(4,128)S(1)} %get-tuple-element.72), channel_id=1, replica_groups=mesh['gy'=4,'gx'=8] {'gx'}, dimensions={0} | all-to-all | bytes 262144 | tf_op jit(solution)/shard_map/all_to_all | solution.py:456
  163.2 13.8 %post.6 = (bf16[2,4,1024,256]{3,2,1,0:T(8,128)(2,1)}, bf16[2,4,1024,256]{3,2,1,0:T(8,128)(2,1)}, f32[2,48,512]{2,1,0:T(8,128)S(1)}, f32[4,4,512]{2,1,0:T(4,128)}...) custom-call(f32[2,4,256,1024]{3,2,1,0:T(8,128)} %get-tuple-element.67.refs_0_, ...), custom_call_target="tpu_custom_call" | custom-call | tf_op jit(solution)/shard_map/post/pallas_call | solution.py:497
  177.0 1.4 copy-done.4
  178.3 1.3 copy-done.6
  179.7 5.1 %all-to-all-start.6 = ((f32[4,4,512]{2,1,0:T(4,128)}), f32[4,4,512]{2,1,0:T(4,128)S(1)}, u32[]{:S(2)}, u32[]{:S(2)}) async-start(f32[4,4,512]{2,1,0:T(4,128)} %get-tuple-element.78), calls=%async_computation.6 | async-start | bytes 65536 | tf_op jit(solution)/shard_map/all_to_all | solution.py:454
  184.8 19.3 %local.7 = (f32[2,4,256,1024]{3,2,1,0:T(8,128)}, f32[2,32,1024]{2,1,0:T(8,128)S(1)}) custom-call(bf16[2,4,1024,256]{3,2,1,0:T(8,128)(2,1)} %get-tuple-element.74.t_hi, bf16[2,4,1024,256]{3,2,1,0:T(8,128)(2,1)} %get-tuple-element.75.t_lo, f32[2,48,512]{2,1,0:T(8,128)S(1)} %get-tuple-element.76.y_state, bf16[256,256]{1,0:T(8,128)(2,1)S(1)} %copy.29.my_hi, ...), custom_call_target="tpu_custom_call" | custom-call | tf_op jit(solution)/shard_map/local/pallas_call | solution.py:453
  204.0 2.3 link.7
  206.3 7.9 %all_to_all.42.refs_3_ = f32[8,4,1024]{2,1,0:T(4,128)S(1)} all-to-all(f32[8,4,1024]{2,1,0:T(4,128)S(1)} %get-tuple-element.82), channel_id=1, replica_groups=mesh['gy'=4,'gx'=8] {'gx'}, dimensions={0} | all-to-all | bytes 262144 | tf_op jit(solution)/shard_map/all_to_all | solution.py:456
  214.2 11.1 %post.7 = (f32[2,1,512,1024]{3,2,1,0:T(8,128)}, f32[2,1,512,1024]{3,2,1,0:T(8,128)}, f32[512,1024]{1,0:T(8,128)S(1)}) custom-call(f32[2,4,256,1024]{3,2,1,0:T(8,128)} %get-tuple-element.77.refs_0_, f32[2,4,8,1024]{3,2,1,0:T(8,128)S(1)} %get-tuple-element.80.refs_1_, f32[2,8,1024]{2,1,0:T(8,128)S(1)} %get-tuple-element.81.refs_2_, ...), custom_call_target="tpu_custom_call" | custom-call | tf_op jit(solution)/shard_map/post/pallas_call | solution.py:497
  225.4 4.0 %pad_maximum_fusion = f32[4,512,1024]{2,1,0:T(8,128)} fusion(f32[1,512,1024]{2,1,0:T(8,128)S(1)} %bitcast.86, f32[1,512,1024]{2,1,0:T(8,128)S(1)} %bitcast.84, f32[1,512,1024]{2,1,0:T(8,128)S(1)} %bitcast.85, f32[1,512,1024]{2,1,0:T(8,128)S(1)} %bitcast.87), kind=kLoop, calls=%fused_computation | loop fusion | flops 6291456 | bytes 16777216 | tf_op jit(solution)/shard_map/stack | solution.py:518
  (104 shorter events, 2.9 us)
Async XLA Ops:
  6.2 8.6 %copy-start.17 = (f32[2,1,128]{2,1,0:T(1,128)}, f32[2,1,128]{2,1,0:T(1,128)S(1)}, u32[]{:S(2)}) copy-start(f32[2,1,128]{2,1,0:T(1,128)S(1)} %pad_maximum_fusion.16.table.refs_8_) | copy-start | bytes 3076
  6.4 17.0 %copy-start.20 = (f32[128,128]{0,1:T(8,128)S(1)}, f32[128,128]{0,1:T(8,128)}, u32[]{:S(2)}) copy-start(f32[128,128]{0,1:T(8,128)} %constant.27) | copy-start | bytes 196612
  6.4 17.0 %copy-start.25 = (pred[128,128]{0,1:T(32,128)(4,1)S(1)}, pred[128,128]{0,1:T(32,128)(4,1)}, u32[]{:S(2)}) copy-start(pred[128,128]{0,1:T(32,128)(4,1)} %constant.48.clone) | copy-start | bytes 49156
  6.4 17.4 %copy-start.31 = (f32[2,128]{1,0:T(2,128)S(1)}, f32[2,128]{1,0:T(2,128)}, u32[]{:S(2)}) copy-start(f32[2,128]{1,0:T(2,128)} %constant.28) | copy-start | bytes 3076
  6.4 17.5 %copy-start.27 = (f32[1024]{0:T(1024)S(1)}, f32[1024]{0:T(1024)}, u32[]{:S(2)}) copy-start(f32[1024]{0:T(1024)} %constant.60) | copy-start | bytes 12292
  6.4 17.5 %copy-start.28 = (f32[1024]{0:T(1024)S(1)}, f32[1024]{0:T(1024)}, u32[]{:S(2)}) copy-start(f32[1024]{0:T(1024)} %constant.59) | copy-start | bytes 12292
  6.4 18.1 %copy-start.22 = (f32[10,512]{1,0:T(8,128)S(1)}, f32[10,512]{1,0:T(8,128)}, u32[]{:S(2)}) copy-start(f32[10,512]{1,0:T(8,128)} %constant.58) | copy-start | bytes 61444
  6.4 18.1 %copy-start.26 = (pred[10,512]{1,0:T(8,128)(4,1)S(1)}, pred[10,512]{1,0:T(8,128)(4,1)}, u32[]{:S(2)}) copy-start(pred[10,512]{1,0:T(8,128)(4,1)} %constant.52.clone) | copy-start | bytes 15364
  6.4 18.8 %copy-start.29 = (f32[512]{0:T(512)S(1)}, f32[512]{0:T(512)}, u32[]{:S(2)}) copy-start(f32[512]{0:T(512)} %constant.62) | copy-start | bytes 6148
  6.5 18.8 %copy-start.30 = (f32[512]{0:T(512)S(1)}, f32[512]{0:T(512)}, u32[]{:S(2)}) copy-start(f32[512]{0:T(512)} %constant.61) | copy-start | bytes 6148
  14.8 2.0 copy-start.1
  16.8 30.6 %all-to-all-start = ((f32[4,4,512]{2,1,0:T(4,128)}), f32[4,4,512]{2,1,0:T(4,128)S(1)}, u32[]{:S(2)}, u32[]{:S(2)}) async-start(f32[4,4,512]{2,1,0:T(4,128)} %get-tuple-element.50), calls=%async_computation | async-start | bytes 65536 | tf_op jit(solution)/shard_map/all_to_all | solution.py:454
  23.9 0.6 copy-start.21
  25.9 0.6 copy-start.23
  25.9 0.6 copy-start.24
  46.7 0.7 copy-start.8
  47.4 1.0 copy-start.9
  50.6 0.7 copy-start.14
  51.3 3.7 %copy-start.15 = (f32[2,8,1024]{2,1,0:T(8,128)}, f32[2,8,1024]{2,1,0:T(8,128)S(1)}, u32[]{:S(2)}) copy-start(f32[2,8,1024]{2,1,0:T(8,128)S(1)} %get-tuple-element.53.refs_2_) | copy-start | bytes 196612
  51.3 9.3 %all-to-all-start.1 = ((f32[8,4,1024]{2,1,0:T(4,128)}), f32[8,4,1024]{2,1,0:T(4,128)S(1)}, u32[]{:S(2)}, u32[]{:S(2)}) async-start(f32[8,4,1024]{2,1,0:T(4,128)} %copy-done.14), calls=%async_computation.1 | async-start | bytes 262144 | tf_op jit(solution)/shard_map/all_to_all | solution.py:456
  60.5 0.8 copy-start.16
  61.4 0.7 copy-start.18
  74.2 2.0 copy-start
  76.2 0.7 copy-start.10
  76.8 0.6 copy-start.19
  77.5 25.3 %all-to-all-start.2 = ((f32[4,4,512]{2,1,0:T(4,128)}), f32[4,4,512]{2,1,0:T(4,128)S(1)}, u32[]{:S(2)}, u32[]{:S(2)}) async-start(f32[4,4,512]{2,1,0:T(4,128)} %copy-done.19), calls=%async_computation.2 | async-start | bytes 65536 | tf_op jit(solution)/shard_map/all_to_all | solution.py:454
  82.5 0.9 copy-start.11
  125.7 1.3 copy-start.2
  127.0 0.7 copy-start.12
  127.7 25.3 %all-to-all-start.4 = ((f32[4,4,512]{2,1,0:T(4,128)}), f32[4,4,512]{2,1,0:T(4,128)S(1)}, u32[]{:S(2)}, u32[]{:S(2)}) async-start(f32[4,4,512]{2,1,0:T(4,128)} %get-tuple-element.68), calls=%async_computation.4 | async-start | bytes 65536 | tf_op jit(solution)/shard_map/all_to_all | solution.py:454
  132.8 0.9 copy-start.13
  177.0 1.4 copy-start.4
  178.3 1.3 copy-start.6
  179.7 24.4 %all-to-all-start.6 = ((f32[4,4,512]{2,1,0:T(4,128)}), f32[4,4,512]{2,1,0:T(4,128)S(1)}, u32[]{:S(2)}, u32[]{:S(2)}) async-start(f32[4,4,512]{2,1,0:T(4,128)} %get-tuple-element.78), calls=%async_computation.6 | async-start | bytes 65536 | tf_op jit(solution)/shard_map/all_to_all | solution.py:454
  214.2 11.1 %copy-start.3 = (f32[512,1024]{1,0:T(8,128)S(1)}, f32[512,1024]{1,0:T(8,128)}, u32[]{:S(2)}) copy-start(f32[512,1024]{1,0:T(8,128)} %copy-done.2) | copy-start | bytes 6291460
  214.2 11.1 %copy-start.5 = (f32[512,1024]{1,0:T(8,128)S(1)}, f32[512,1024]{1,0:T(8,128)}, u32[]{:S(2)}) copy-start(f32[512,1024]{1,0:T(8,128)} %copy-done.4) | copy-start | bytes 6291460
  214.2 11.1 %copy-start.7 = (f32[512,1024]{1,0:T(8,128)S(1)}, f32[512,1024]{1,0:T(8,128)}, u32[]{:S(2)}) copy-start(f32[512,1024]{1,0:T(8,128)} %copy-done.6) | copy-start | bytes 6291460

commit v2 on v1

--- a/solution.py
+++ b/solution.py
@@ -13,7 +13,7 @@
 F32 = jnp.float32
 BF16 = jnp.bfloat16
 HIGHEST = lax.Precision.HIGHEST
-VMEM_LIMIT = 48 * 1024 * 1024
+MIB = 1024 * 1024
 
 
 def complex_mul(a, b):
@@ -97,20 +97,42 @@
     return real_rows((jnp.where(masks, re, 0.0), jnp.where(masks, im, 0.0)))
 
 
+def partner(mine, slot, count, way):
+    if count & (count - 1) == 0:
+        return mine ^ slot
+    return (mine + way * slot) % count
+
+
+def exchange(pieces, axis):
+    count = len(pieces)
+    got = [pieces[0]]
+    for s in range(1, count):
+        pairs = [(d, partner(d, s, count, 1)) for d in range(count)]
+        got.append(lax.ppermute(pieces[s], axis, pairs))
+    return got
+
+
 def link_coefs(modulus, angle, off, end, count, mine, length):
-    other = jnp.arange(count, dtype=jnp.int32)
-    far = root_powers(modulus, angle, length * (2 * count - 2 - mine - other))
-    near = root_powers(modulus, angle, length * jnp.maximum(jnp.abs(other - mine) - 1, 0))
+    slots = np.arange(count, dtype=np.int32)
     root = (modulus * jnp.cos(angle), modulus * jnp.sin(angle))
-    tail = complex_mul(end, far)
+    one = jnp.ones((count,), F32)
+    zero = jnp.zeros((count,), F32)
+
+    def factors(other):
+        far = root_powers(modulus, angle, length * (2 * count - 2 - mine - other))
+        near = root_powers(modulus, angle, length * jnp.maximum(jnp.abs(other - mine) - 1, 0))
+        return near, complex_mul(end, far)
+
+    other = partner(mine, slots, count, 1)
+    near, tail = factors(other)
     head = complex_mul(complex_mul(off, root), near)
     before = other < mine
-    one = jnp.ones((count,), F32)
-    zero = jnp.zeros((count,), F32)
     send_f = (jnp.where(before, tail[0], one), jnp.where(before, tail[1], zero))
     send_b = (jnp.where(before, head[0], zero), jnp.where(before, head[1], zero))
+    other = partner(mine, slots, count, -1)
+    near, tail = factors(other)
+    before, after = other < mine, other > mine
     recv_f = (jnp.where(before, near[0], zero), jnp.where(before, near[1], zero))
-    after = other > mine
     recv_b = (jnp.where(after, one, tail[0]), jnp.where(after, zero, tail[1]))
     return jnp.stack([*send_f, *send_b, *recv_f, *recv_b], axis=1)
 
@@ -155,7 +177,7 @@
 def gather_entries(coef, recv, count, chain):
     first = second = None
     for e in range(count):
-        pair = (recv[e, 2 * chain : 2 * chain + 1, :], recv[e, 2 * chain + 1 : 2 * chain + 2, :])
+        pair = (recv[e][2 * chain : 2 * chain + 1, :], recv[e][2 * chain + 1 : 2 * chain + 2, :])
         first = add_pair(first, weigh(coef, e, 4, pair))
         second = add_pair(second, weigh(coef, e, 6, pair))
     return first, second
@@ -164,8 +186,8 @@
 def write_pieces(coef, pieces, count, chain, f_pair, b_pair):
     for e in range(count):
         out = add_pair(weigh(coef, e, 0, f_pair), weigh(coef, e, 2, b_pair))
-        pieces[e, 2 * chain : 2 * chain + 1, :] = out[0]
-        pieces[e, 2 * chain + 1 : 2 * chain + 2, :] = out[1]
+        pieces[e][2 * chain : 2 * chain + 1, :] = out[0]
+        pieces[e][2 * chain + 1 : 2 * chain + 2, :] = out[1]
 
 
 def put_turned(t_hi, t_lo, chain, b, pair):
@@ -175,62 +197,74 @@
         t_lo[chain, 0, b * W : (b + 1) * W, part * W : (part + 1) * W] = lo
 
 
-def y_states(t_hi, t_lo, st3, st_hi, coef_y, y_state, y_pieces, nby, county):
-    rows = st_hi.shape[0]
+def add_states(acc, t_hi, t_lo, st, b):
+    rows = slice(b * W, (b + 1) * W)
+    high = jnp.concatenate([t_hi[0, 0, rows, :], t_hi[1, 0, rows, :]], axis=0)
+    low = jnp.concatenate([t_lo[0, 0, rows, :], t_lo[1, 0, rows, :]], axis=0)
+    part = nn(jnp.concatenate([high, low], axis=1), st[b])
+    return part if acc is None else acc + part
+
+
+def put_states(acc, coef_y, y_state, y_pieces, nby, county):
+    half = acc.shape[1] // 2
+    rows = y_state.shape[2]
+    turned = acc.T
+    both = turned[:rows] + turned[half : half + rows]
+    d = 4 * nby
     for chain in range(2):
-        acc = jnp.zeros((2 * rows, W), F32)
-        low = jnp.zeros((rows, W), F32)
-        for b in range(nby):
-            lanes = slice(2 * W * b, 2 * W * (b + 1))
-            acc = acc + nt(st3[:, lanes], t_hi[chain, 0, b * W : (b + 1) * W, :])
-            low = low + nt(st_hi[:, lanes], t_lo[chain, 0, b * W : (b + 1) * W, :])
-        total = acc[:rows] + acc[rows:] + low
-        y_state[chain] = total
-        d = 4 * nby
+        total = both[:, chain * W : (chain + 1) * W]
+        y_state[chain, 0] = total
         write_pieces(
             coef_y, y_pieces, county, chain,
             (total[d : d + 1], total[d + 1 : d + 2]), (total[d + 2 : d + 3], total[d + 3 : d + 4]),
         )
 
 
-def first_kernel(nby, county, src, rec, idx, table, st3, st_hi, coef_y, t_hi, t_lo, y_state, y_pieces):
+def first_kernel(nby, county, src, rec, idx, table, st, coef_y, early, t_hi, t_lo, y_state, *y_pieces):
+    acc = None
     for b in range(nby):
         lanes = slice(b * W, (b + 1) * W)
         put_turned(t_hi, t_lo, 0, b, (src[0, 0, :, lanes], src[1, 0, :, lanes]))
         index = idx[0, :, lanes]
         cos, sin = lookup(table[0], index), lookup(table[1], index)
         put_turned(t_hi, t_lo, 1, b, complex_mul((rec[0, 0, :, lanes], -rec[1, 0, :, lanes]), (cos, sin)))
-    y_states(t_hi, t_lo, st3, st_hi, coef_y, y_state, y_pieces, nby, county)
-
-
-def local_kernel(nby, t_hi, t_lo, y_state, my_hi, my_lo, sp_y, lx_h, lx_l, w_out, x_state, vx_hi, vx_lo):
-    a = pl.program_id(1)
-    srows = lx_l.shape[1] - 2 * W
-    main = nn(t_hi[0, 0], my_hi[...]) + nn(t_hi[0, 0], my_lo[...]) + nn(t_lo[0, 0], my_hi[...])
-    for b in range(nby):
-        st = split3(y_state[0, 4 * b : 4 * b + 4, :], True)
-        v = main[b * W : (b + 1) * W] + tn(st, sp_y[...])
-        hi, lo = halves(v)
-        for part in range(2):
-            vx_hi[part * W : (part + 1) * W, b * W : (b + 1) * W] = hi[:, part * W : (part + 1) * W]
-            vx_lo[part * W : (part + 1) * W, b * W : (b + 1) * W] = lo[:, part * W : (part + 1) * W]
-    high = nn(lx_h[0], vx_hi[...])
-    low = nn(lx_l[0], vx_lo[...])
-    w_out[0, 0] = high[: 2 * W] + high[2 * W : 4 * W] + low[: 2 * W]
-    states = high[4 * W : 4 * W + srows] + high[4 * W + srows :] + low[2 * W :]
-
-    @pl.when(a == 0)
-    def _():
-        x_state[0] = states
-
-    @pl.when(a > 0)
-    def _():
-        x_state[0] += states
+        acc = add_states(acc, t_hi, t_lo, st, b)
+    put_states(acc, coef_y, y_state, y_pieces, nby, county)
+
+
+def local_kernel(nbx, nby, t_hi, t_lo, y_state, my3, sp_y, lx, w_out, x_state, vx_hi, vx_lo):
+    x_state[...] = jnp.zeros_like(x_state)
+
+    def block(i, carry):
+        c, a = i // nbx, i % nbx
+        state = y_state[c, a]
+        for j in range(0, nby, 2):
+            rows = slice(j * W, (j + 2) * W)
+            high, low = t_hi[c, a, rows, :], t_lo[c, a, rows, :]
+            main = nn(jnp.concatenate([high, low, high], axis=1), my3[...])
+            for b in (j, j + 1):
+                v = main[(b - j) * W : (b - j + 1) * W] + tn(split3(state[4 * b : 4 * b + 4, :], True), sp_y[...])
+                hi, lo = halves(v)
+                for part in range(2):
+                    at = slice(part * W, (part + 1) * W)
+                    vx_hi[at, b * W : (b + 1) * W] = hi[:, at]
+                    vx_lo[at, b * W : (b + 1) * W] = lo[:, at]
+        left = lx[a]
+        for j in range(0, nby, 2):
+            lanes = slice(j * W, (j + 2) * W)
+            high, low = vx_hi[:, lanes], vx_lo[:, lanes]
+            out = nn(left, jnp.concatenate([high, low, high], axis=0))
+            w_out[c, a, :, lanes] = out[: 2 * W]
+            x_state[c, :, lanes] += out[2 * W :]
+        return carry
+
+    lax.fori_loop(0, 2 * nbx, block, 0)
 
 
 def link_kernel(
-    nbx, county, countx, recv_y, x_local, coef_y, coef_x, sx, edge, mxt, x_state, ym, x_pieces
+    nbx, county, countx, x_local, coef_y, coef_x, sx, edge, mxt, *refs
 ):
+    recv_y, (x_state, ym), x_pieces = refs[:county], refs[county : county + 2], refs[county + 2 :]
     for chain in range(2):
         (fr, fi), (br, bi) = gather_entries(coef_y, recv_y, county, chain)
         cols = []
@@ -267,19 +301,37 @@
 def post_kernel(plan, nby, county, countx, *refs):
     refs = list(refs)
     take = lambda: refs.pop(0)
-    w_in, x_state, ym, recv_x, coef_x, edge, sp_x, sp_dev, table = (take() for _ in range(9))
+    w_in, x_state, ym, coef_x, edge, sp_x, sp_dev, table = (take() for _ in range(8))
+    recv_x = [take() for _ in range(countx)]
     idx_s = take()
     idx_r = take() if plan["turn"] else None
-    st3, st_hi, coef_y = (take(), take(), take()) if plan["turn"] else (None,) * 3
+    st, coef_y = (take(), take()) if plan["turn"] else (None, None)
     olds = [{"s": (take(), take()) if z[1] == "split" else take() if z[1] == "field" else None,
              "r": take() if z[2] else None} for z in plan["images"]]
+    if plan["alias"]:
+        take()
     if plan["turn"]:
-        t_hi, t_lo, y_state, y_pieces = (take() for _ in range(4))
+        t_hi, t_lo, y_state = (take() for _ in range(3))
+        y_pieces = [take() for _ in range(county)]
     else:
         src_out, rec_out = take(), take()
     keep_out = take() if plan["keep"] else None
-    image_outs = [take() for _ in plan["images"]]
-
+    image = take() if plan["images"] else None
+    if plan["images"]:
+        slots, sems = take(), take()
+    a, last = pl.program_id(0), pl.num_programs(0) - 1
+    slot = lax.rem(a, 2)
+
+    def image_copy(n, at, slot):
+        rows = pl.ds(pl.multiple_of(at * W, W), W)
+        return pltpu.make_async_copy(slots.at[n, slot], image.at[plan["images"][n][0], rows], sems.at[n, slot])
+
+    for n in range(len(plan["images"])):
+        @pl.when(a >= 2)
+        def _():
+            image_copy(n, a - 2, slot).wait()
+
+    acc = None
     lefts, rights = [], []
     for chain in range(2):
         first, second = gather_entries(coef_x, recv_x, countx, chain)
@@ -290,9 +342,12 @@
         lefts.append(split3(left, True))
     for b in range(nby):
         lanes = slice(b * W, (b + 1) * W)
+        if b % 2 == 0:
+            wide = slice(b * W, min(b + 2, nby) * W)
+            fixes = [tn(lefts[chain], rights[chain][:, wide]) for chain in range(2)]
         fields = []
         for chain in range(2):
-            u = w_in[chain, 0, :, lanes] + tn(lefts[chain], rights[chain][:, lanes])
+            u = w_in[chain, 0, :, lanes] + fixes[chain][:, b % 2 * W : (b % 2 + 1) * W]
             fields.append((u[:W], u[W:]))
         index = idx_s[0, :, lanes]
         source = complex_mul(fields[0], (lookup(table[0], index), lookup(table[1], index)))
@@ -301,12 +356,13 @@
             put_turned(t_hi, t_lo, 0, b, source)
             index = idx_r[0, :, lanes]
             put_turned(t_hi, t_lo, 1, b, complex_mul(back, (lookup(table[0], index), lookup(table[1], index))))
+            acc = add_states(acc, t_hi, t_lo, st, b)
         else:
             src_out[0, 0, :, lanes], src_out[1, 0, :, lanes] = source
             rec_out[0, 0, :, lanes], rec_out[1, 0, :, lanes] = back[0], -back[1]
         if keep_out is not None:
             keep_out[0, :, lanes], keep_out[1, :, lanes] = back
-        for old, (_, how, has_r), out in zip(olds, plan["images"], image_outs):
+        for n, (old, (_, how, has_r)) in enumerate(zip(olds, plan["images"])):
             if how == "split":
                 hi, lo = old["s"]
                 rows = slice(b * W, (b + 1) * W)
@@ -317,9 +373,19 @@
             else:
                 s = source
             r = (old["r"][0, :, lanes], old["r"][1, :, lanes]) if has_r else back
-            out[:, lanes] = s[0] * r[0] - s[1] * r[1]
+            slots[n, slot, :, lanes] = s[0] * r[0] - s[1] * r[1]
     if plan["turn"]:
-        y_states(t_hi, t_lo, st3, st_hi, coef_y, y_state, y_pieces, nby, county)
+        put_states(acc, coef_y, y_state, y_pieces, nby, county)
+    for n in range(len(plan["images"])):
+        image_copy(n, a, slot).start()
+
+        @pl.when((a == last) & (a >= 1))
+        def _():
+            image_copy(n, a - 1, 1 - slot).wait()
+
+        @pl.when(a == last)
+        def _():
+            image_copy(n, a, slot).wait()
 
 
 def whole(shape):
@@ -327,10 +393,15 @@
 
 
 SMEM = pl.BlockSpec(memory_space=pltpu.SMEM)
-
-
-def params(dims):
-    return pltpu.CompilerParams(vmem_limit_bytes=VMEM_LIMIT, dimension_semantics=("arbitrary",) * dims)
+VMEM = pl.BlockSpec(memory_space=pltpu.VMEM)
+
+
+def in_hbm(x):
+    return pltpu.with_memory_space_constraint(x, pltpu.HBM)
+
+
+def params(mib):
+    return pltpu.CompilerParams(vmem_limit_bytes=mib * MIB)
 
 
 def on_device(source_field, receiver_field, velocity_index, slowness, freq_index, root_modulus, root_angle):
@@ -359,14 +430,16 @@
 
     rows_y = -(-(4 * nby + 4) // 16) * 16
     rows_x = -(-(4 * nbx + 4) // 16) * 16
-    st_hi, st_lo = rounded_halves(pad_rows(state_matrix(modulus, angle, len_y), rows_y))
-    st3 = jnp.concatenate([st_hi, st_lo], axis=0)
+    st_hi, st_lo = rounded_halves(pad_rows(state_matrix(modulus, angle, len_y), -(-rows_y // 64) * 64))
+    st = jnp.concatenate([jnp.concatenate([st_hi, st_lo], axis=0), jnp.concatenate([st_hi, 0 * st_lo], axis=0)], axis=1)
+    st = st.reshape(st.shape[0], 2, nby, 2 * W).transpose(2, 1, 3, 0).reshape(nby, 4 * W, st.shape[0])
     sx = pad_rows(state_matrix(modulus, angle, len_x), rows_x)
     sx_hi, sx_lo = rounded_halves(sx)
-    blocks_of = lambda x: x.reshape(rows_x, nbx, 2 * W).transpose(1, 0, 2)
-    rep = lambda x: jnp.broadcast_to(x[None], (nbx,) + x.shape)
-    lx_h = jnp.concatenate([rep(mx_hi), rep(mx_lo), blocks_of(sx_hi), blocks_of(sx_lo)], axis=1)
-    lx_l = jnp.concatenate([rep(mx_hi), blocks_of(sx_hi)], axis=1)
+    lx = jnp.concatenate([
+        jnp.broadcast_to(jnp.concatenate([mx_hi, mx_hi, mx_lo], axis=1)[None], (nbx, 2 * W, 6 * W)),
+        jnp.concatenate([x.reshape(rows_x, nbx, 2 * W).transpose(1, 0, 2) for x in (sx_hi, sx_hi, sx_lo)], axis=2),
+    ], axis=1)
+    my3 = jnp.concatenate([my_hi, my_hi, my_lo], axis=0)
 
     near = complex_mul(off, root_powers(modulus, angle, jnp.asarray(np.stack([at + 1, W - at]).astype(np.int32))))
     spread = spread_rows(near)
@@ -386,74 +459,66 @@
     coef_y = link_coefs(modulus, angle, off, end, county, lax.axis_index("gy"), len_y)
     coef_x = link_coefs(modulus, angle, off, end, countx, lax.axis_index("gx"), len_x)
 
+    mxt = mx.T
+    (my3, sp_y, lx, sx, edge_y, mxt, spread, edge_x, table, st, coef_y, coef_x) = lax.optimization_barrier(
+        (my3, sp_y, lx, sx, edge_y, mxt, spread, edge_x, table, st, coef_y, coef_x)
+    )
+
     turned = jax.ShapeDtypeStruct((2, nbx, nby * W, 2 * W), BF16)
     turned_spec = pl.BlockSpec((2, 1, nby * W, 2 * W), lambda a: (0, a, 0, 0))
-    y_state_shape = jax.ShapeDtypeStruct((2, rows_y, len_x), F32)
-    y_state_spec = pl.BlockSpec((2, rows_y, W), lambda a: (0, 0, a))
-    y_piece_shape = jax.ShapeDtypeStruct((county, 4, len_x), F32)
-    y_piece_spec = pl.BlockSpec((county, 4, W), lambda a: (0, 0, a))
+    y_state_shape = jax.ShapeDtypeStruct((2, nbx, rows_y, W), F32)
+    y_state_spec = pl.BlockSpec((2, 1, rows_y, W), lambda a: (0, a, 0, 0))
+    y_piece_shape = jax.ShapeDtypeStruct((4, len_x), F32)
+    y_piece_spec = pl.BlockSpec((4, W), lambda a: (0, a))
     field_spec = pl.BlockSpec((2, 1, W, len_y), lambda a: (0, 0, a, 0))
     keep_spec = pl.BlockSpec((2, W, len_y), lambda a: (0, a, 0))
-    image_spec = pl.BlockSpec((W, len_y), lambda a: (a, 0))
     level_spec = lambda z: pl.BlockSpec((1, W, len_y), lambda a: (z, a, 0))
-    turn_out = [turned, turned, y_state_shape, y_piece_shape]
-    turn_specs = [turned_spec, turned_spec, y_state_spec, y_piece_spec]
-
-    t_hi, t_lo, y_state, y_pieces = pl.pallas_call(
+    turn_out = [turned, turned, y_state_shape] + [y_piece_shape] * county
+    turn_specs = [turned_spec, turned_spec, y_state_spec] + [y_piece_spec] * county
+
+    t_hi, t_lo, y_state, *y_pieces = pl.pallas_call(
         functools.partial(first_kernel, nby, county),
         grid=(nbx,),
-        in_specs=[field_spec, field_spec, level_spec(depth - 1), whole(table.shape), whole(st3.shape),
-                  whole(st_hi.shape), SMEM],
+        in_specs=[field_spec, field_spec, level_spec(depth - 1), whole(table.shape), whole(st.shape), SMEM, pl.BlockSpec(memory_space=pl.ANY)],
         out_specs=turn_specs,
         out_shape=turn_out,
-        compiler_params=params(1),
+        compiler_params=params(20),
         name="first",
-    )(source_field, receiver_field, velocity_index, table, st3, st_hi, coef_y)
+    )(in_hbm(source_field), in_hbm(receiver_field), in_hbm(velocity_index), table, st, coef_y, my3)
 
     local = pl.pallas_call(
-        functools.partial(local_kernel, nby),
-        grid=(2, nbx),
-        in_specs=[
-            pl.BlockSpec((1, 1, nby * W, 2 * W), lambda c, a: (c, a, 0, 0)),
-            pl.BlockSpec((1, 1, nby * W, 2 * W), lambda c, a: (c, a, 0, 0)),
-            pl.BlockSpec((1, rows_y, W), lambda c, a: (c, 0, a)),
-            whole(my_hi.shape), whole(my_lo.shape), whole(sp_y.shape),
-            pl.BlockSpec((1,) + lx_h.shape[1:], lambda c, a: (a, 0, 0)),
-            pl.BlockSpec((1,) + lx_l.shape[1:], lambda c, a: (a, 0, 0)),
-        ],
-        out_specs=[
-            pl.BlockSpec((1, 1, 2 * W, len_y), lambda c, a: (c, a, 0, 0)),
-            pl.BlockSpec((1, rows_x, len_y), lambda c, a: (c, 0, 0)),
-        ],
+        functools.partial(local_kernel, nbx, nby),
+        in_specs=[VMEM] * 6,
+        out_specs=[VMEM] * 2,
         out_shape=[
             jax.ShapeDtypeStruct((2, nbx, 2 * W, len_y), F32),
             jax.ShapeDtypeStruct((2, rows_x, len_y), F32),
         ],
         scratch_shapes=[pltpu.VMEM((2 * W, len_y), BF16)] * 2,
-        compiler_params=params(2),
+        compiler_params=params(16),
         name="local",
     )
 
     link = pl.pallas_call(
         functools.partial(link_kernel, nbx, county, countx),
-        in_specs=[pl.BlockSpec(memory_space=pltpu.VMEM)] * 2 + [SMEM] * 2 + [pl.BlockSpec(memory_space=pltpu.VMEM)] * 3,
+        in_specs=[VMEM] + [SMEM] * 2 + [VMEM] * (3 + county),
+        out_specs=[VMEM] * (2 + countx),
         out_shape=[
             jax.ShapeDtypeStruct((2, nbx, 8, len_y), F32),
             jax.ShapeDtypeStruct((2, 8, 2 * len_x), F32),
-            jax.ShapeDtypeStruct((countx, 4, len_y), F32),
-        ],
-        compiler_params=params(0),
+        ] + [jax.ShapeDtypeStruct((4, len_y), F32)] * countx,
+        compiler_params=params(8),
         name="link",
     )
 
     source_levels = {0: ("field", (source_field,))}
     kept = {}
-    images = [None] * depth
+    image = None
     for step in range(depth):
-        w, x_local = local(t_hi, t_lo, y_state, my_hi, my_lo, sp_y, lx_h, lx_l)
-        recv_y = lax.all_to_all(y_pieces, "gy", 0, 0)
-        x_state, ym, x_pieces = link(recv_y, x_local, coef_y, coef_x, sx, edge_y, mx.T)
-        recv_x = lax.all_to_all(x_pieces, "gx", 0, 0)
+        w, x_local = local(t_hi, t_lo, y_state, my3, sp_y, lx)
+        recv_y = exchange(y_pieces, "gy")
+        x_state, ym, *x_pieces = link(x_local, coef_y, coef_x, sx, edge_y, mxt, *recv_y)
+        recv_x = exchange(x_pieces, "gx")
         turn = step < depth - 1
         level_r = depth - 1 - step
         todo = [z for z in range(depth) if max(z - 1, depth - 1 - z) == step]
@@ -462,60 +527,70 @@
             "keep": level_r - 1 > step,
             "images": [(z, None if z - 1 == step else source_levels[z][0], z != level_r) for z in todo],
         }
-        args = [w, x_state, ym, recv_x, coef_x, edge_y, spread, edge_x, table, velocity_index]
+        args = [w, x_state, ym, coef_x, edge_y, spread, edge_x, table, *recv_x, in_hbm(velocity_index)]
         specs = [
             pl.BlockSpec((2, 1, 2 * W, len_y), lambda a: (0, a, 0, 0)),
             pl.BlockSpec((2, 1, 8, len_y), lambda a: (0, a, 0, 0)),
             pl.BlockSpec((2, 8, 2 * W), lambda a: (0, 0, a)),
-            whole(recv_x.shape), SMEM, whole(edge_y.shape), whole(spread.shape),
+            SMEM, whole(edge_y.shape), whole(spread.shape),
             pl.BlockSpec((1, 4, 2 * W), lambda a: (a, 0, 0)),
-            whole(table.shape), level_spec(step),
-        ]
+            whole(table.shape),
+        ] + [whole((4, len_y))] * countx + [level_spec(step)]
         if turn:
-            args += [velocity_index, st3, st_hi, coef_y]
-            specs += [level_spec(depth - 2 - step), whole(st3.shape), whole(st_hi.shape), SMEM]
+            args += [in_hbm(velocity_index), st, coef_y]
+            specs += [level_spec(depth - 2 - step), whole(st.shape), SMEM]
         for z, how, has_r in plan["images"]:
             if how == "split":
-                args += source_levels[z][1]
+                args += [in_hbm(x) for x in source_levels[z][1]]
                 specs += [pl.BlockSpec((1, 1, nby * W, 2 * W), lambda a: (0, a, 0, 0))] * 2
             elif how == "field":
-                args += source_levels[z][1]
+                args += [in_hbm(x) for x in source_levels[z][1]]
                 specs += [field_spec]
             if has_r:
-                args += [kept[z]]
+                args += [in_hbm(kept[z])]
                 specs += [keep_spec]
         if turn:
             shapes, out_specs = list(turn_out), list(turn_specs)
         else:
-            shapes = [jax.ShapeDtypeStruct(source_field.shape, F32)] * 2
+            shapes = [pltpu.HBM(source_field.shape, F32)] * 2
             out_specs = [field_spec] * 2
         if plan["keep"]:
-            shapes.append(jax.ShapeDtypeStruct((2, len_x, len_y), F32))
+            shapes.append(pltpu.HBM((2, len_x, len_y), F32))
             out_specs.append(keep_spec)
-        shapes += [jax.ShapeDtypeStruct((len_x, len_y), F32)] * len(todo)
-        out_specs += [image_spec] * len(todo)
+        aliases, scratch = {}, []
+        if todo:
+            if image is not None:
+                aliases = {len(args): len(shapes)}
+                args += [in_hbm(image)]
+                specs += [pl.BlockSpec(memory_space=pl.ANY)]
+            shapes.append(pltpu.HBM((depth, len_x, len_y), F32))
+            out_specs.append(pl.BlockSpec(memory_space=pl.ANY))
+            scratch = [pltpu.VMEM((len(todo), 2, W, len_y), F32), pltpu.SemaphoreType.DMA((len(todo), 2))]
+        plan["alias"] = bool(aliases)
         outs = pl.pallas_call(
             functools.partial(post_kernel, plan, nby, county, countx),
             grid=(nbx,),
             in_specs=specs,
             out_specs=out_specs,
             out_shape=shapes,
-            compiler_params=params(1),
+            scratch_shapes=scratch,
+            input_output_aliases=aliases,
+            compiler_params=params(20),
             name="post",
         )(*args)
         outs = list(outs)
         if turn:
-            t_hi, t_lo, y_state, y_pieces = outs[:4]
-            outs = outs[4:]
+            t_hi, t_lo, y_state, *y_pieces = outs[: 3 + county]
+            outs = outs[3 + county :]
             source_levels[step + 1] = ("split", (t_hi, t_lo))
         else:
             source, receiver = outs[:2]
             outs = outs[2:]
         if plan["keep"]:
             kept[level_r] = outs.pop(0)
-        for z in todo:
-            images[z] = outs.pop(0)
-    return jnp.stack(images), source, receiver
+        if todo:
+            image = outs.pop(0)
+    return image, source, receiver
 
 
 def solution(mesh):

time: 230 us -> 173 us (0.75)
  Pallas kernels: 144 us -> 102 us
  blocking collectives: 23.8 us -> 0 us
  starting transfers between devices: 25.3 us -> 44.4 us
  local copies, waits for them, and re-layouts: 18.4 us -> 4.67 us
  waiting for transfers between devices: 4.03 us -> 11.8 us
  other arithmetic: 10 us -> 5.55 us
    ppermute x0 -> x40, starting transfers between devices: none -> 44.4 us  [exchange(): got.append(lax.ppermute(pieces[s], axis, pairs))]
    pallas_call x8, Pallas kernels: 86.2 us -> 47.8 us  [the longest x4 38.6 us: on_device(): w, x_local = local(t_hi, t_lo, y_state, my3, sp_y, lx)]
    all_to_all x5 -> x0, starting transfers between devices: 25.3 us -> none  [the longest x4 21.6 us: on_device(): recv_y = lax.all_to_all(y_pieces, 'gy', 0, 0)]
    all_to_all x3 -> x0, blocking collectives: 23.8 us -> none  [on_device(): recv_x = lax.all_to_all(x_pieces, 'gx', 0, 0)]
    unnamed x65 -> x25, local copies, waits for them, and re-layouts: 17.1 us -> 0.07 us
    ppermute x0 -> x40, waiting for transfers between devices: none -> 11.8 us  [exchange(): got.append(lax.ppermute(pieces[s], axis, pairs))]
    all_to_all x5 -> x0, waiting for transfers between devices: 4.03 us -> none  [the longest x1 4.02 us: on_device(): recv_x = lax.all_to_all(x_pieces, 'gx', 0, 0)]
    another operation x1 -> x12, other arithmetic: 4 us -> 0.38 us  [link_coefs(): return jnp.stack([*send_f, *send_b, *recv_f, *recv_b], axis=1)]
  transfers between devices with their start and end apart: 5 -> 40, of which waited for: 1 -> 8; matrix products, arithmetic and copies ran while one was open for 2% -> 0% of each run, Pallas kernels for 34% -> 22%
where the time goes in v2:
time: 173 us; the launch traced here: 172 us
  Pallas kernels  102 us (59%)
  starting transfers between devices  44.4 us (26%)
  waiting for transfers between devices  11.8 us (7%)
  other arithmetic  5.55 us (3%)
  local copies, waits for them, and re-layouts  4.67 us (3%)
  between operations  4.03 us (2%)
    pallas_call x4, Pallas kernels, on_device(): pl.pallas_call(functools.partial(post_kernel, plan, nby, county, countx),...  46.7 us
    ppermute x40, starting transfers between devices, exchange(): got.append(lax.ppermute(pieces[s], axis, pairs))  44.4 us
    pallas_call x4, Pallas kernels, on_device(): w, x_local = local(t_hi, t_lo, y_state, my3, sp_y, lx)  38.6 us
    ppermute x40, waiting for transfers between devices, exchange(): got.append(lax.ppermute(pieces[s], axis, pairs))  11.8 us
    pallas_call x4, Pallas kernels, on_device(): link(x_local, coef_y, coef_x, sx, edge_y, mxt, *recv_y)  9.19 us
    pallas_call x1, Pallas kernels, on_device(): pl.pallas_call(functools.partial(first_kernel, nby, county), grid=(nbx,),...  7.35 us
  transfers between devices with their start and end apart: 40, of which 8 were waited for; matrix products, arithmetic and copies ran while one was open for 0% of the time, Pallas kernels for 22%

profile of v2, /device:TPU:0, one launch (start us, length us, event | category | flops | bytes accessed | tf_op | source)
XLA Modules:
  0.0 172.3 jit_solution(15744816789478175522)
XLA Ops:
  2.5 0.7 fusion.61
  3.3 1.3 multiply_select_fusion
  9.4 0.7 fusion.63
  10.2 0.8 copy.61
  11.4 0.8 pad_maximum_fusion
  12.6 1.2 copy.79.early.my3
  13.8 7.3 %first.1 = (bf16[2,4,1024,256]{3,2,1,0:T(8,128)(2,1)S(1)}, bf16[2,4,1024,256]{3,2,1,0:T(8,128)(2,1)S(1)}, f32[2,4,48,128]{3,2,1,0:T(8,128)S(1)}, f32[4,512]{1,0:...) custom-call(f32[2,1,512,1024]{3,2,1,0:T(8,128)} %refs_17_.7, ...), custom_call_target="tpu_custom_call" | custom-call | tf_op jit(solution)/shard_map/first/pallas_call | solution.py:479
  21.1 3.1 %collective-permute-start = (f32[4,512]{1,0:T(4,128)S(1)}, f32[4,512]{1,0:T(4,128)S(1)}, u32[]{:S(2)}, u32[]{:S(2)}) collective-permute-start(f32[4,512]{1,0:T(4,128)S(1)} %get-tuple-element.113), channel_id=1, source_target_pairs={{0,8},{8,0},{16,24},{24,16},{1,9},{9,1},{17,25},{25,17},{2,10},{10... | collective-permute-start | bytes 24584 | tf_op jit(solution)/shard_map/ppermute | solution.py:111
  24.2 2.6 %collective-permute-start.1 = (f32[4,512]{1,0:T(4,128)S(1)}, f32[4,512]{1,0:T(4,128)S(1)}, u32[]{:S(2)}, u32[]{:S(2)}) collective-permute-start(f32[4,512]{1,0:T(4,128)S(1)} %get-tuple-element.114), channel_id=1, source_target_pairs={{0,16},{8,24},{16,0},{24,8},{1,17},{9,25},{17,1},{25,9},{2,18},{10... | collective-permute-start | bytes 24584 | tf_op jit(solution)/shard_map/ppermute | solution.py:111
  26.8 9.6 %local.4 = (f32[2,4,256,1024]{3,2,1,0:T(8,128)S(1)}, f32[2,32,1024]{2,1,0:T(8,128)S(1)}) custom-call(bf16[2,4,1024,256]{3,2,1,0:T(8,128)(2,1)S(1)} %get-tuple-element.101.t_hi, bf16[2,4,1024,256]{3,2,1,0:T(8,128)(2,1)S(1)} %get-tuple-element.102.t_lo, f32[2,4,48,128]{3,2,1,0:T(8,128)S(1)} %get-tuple-element.103.y_state, ...), custom_call_target="tpu_custom_call" | custom-call | tf_op jit(solution)/shard_map/local/pallas_call | solution.py:518
  36.5 2.3 %link.4 = (f32[2,4,8,1024]{3,2,1,0:T(8,128)S(1)}, f32[2,8,1024]{2,1,0:T(8,128)S(1)}, f32[4,1024]{1,0:T(4,128)S(1)}, f32[4,1024]{1,0:T(4,128)S(1)}, f32[4,1024]{1...) custom-call(f32[2,32,1024]{2,1,0:T(8,128)S(1)} %get-tuple-element.10, ...), custom_call_target="tpu_custom_call" | custom-call | tf_op jit(solution)/shard_map/link/pallas_call | solution.py:520
  38.9 1.8 %collective-permute-start.4 = (f32[4,1024]{1,0:T(4,128)S(1)}, f32[4,1024]{1,0:T(4,128)S(1)}, u32[]{:S(2)}, u32[]{:S(2)}) collective-permute-start(f32[4,1024]{1,0:T(4,128)S(1)} %get-tuple-element.122), channel_id=1, source_target_pairs={{0,2},{1,3},{2,0},{3,1},{4,6},{5,7},{6,4},{7,5},{8,10},{9,11},{10,... | collective-permute-start | bytes 49160 | tf_op jit(solution)/shard_map/ppermute | solution.py:111
  40.8 1.7 %collective-permute-start.6 = (f32[4,1024]{1,0:T(4,128)S(1)}, f32[4,1024]{1,0:T(4,128)S(1)}, u32[]{:S(2)}, u32[]{:S(2)}) collective-permute-start(f32[4,1024]{1,0:T(4,128)S(1)} %get-tuple-element.124), channel_id=1, source_target_pairs={{0,4},{1,5},{2,6},{3,7},{4,0},{5,1},{6,2},{7,3},{8,12},{9,13},{10,... | collective-permute-start | bytes 49160 | tf_op jit(solution)/shard_map/ppermute | solution.py:111
  42.5 2.6 %collective-permute-start.8 = (f32[4,1024]{1,0:T(4,128)S(1)}, f32[4,1024]{1,0:T(4,128)S(1)}, u32[]{:S(2)}, u32[]{:S(2)}) collective-permute-start(f32[4,1024]{1,0:T(4,128)S(1)} %get-tuple-element.126), channel_id=1, source_target_pairs={{0,6},{1,7},{2,4},{3,5},{4,2},{5,3},{6,0},{7,1},{8,14},{9,15},{10,... | collective-permute-start | bytes 49160 | tf_op jit(solution)/shard_map/ppermute | solution.py:111
  45.7 1.5 collective-permute-done.8.refs_14_
  47.2 2.0 %collective-permute-done.9.refs_15_ = f32[4,1024]{1,0:T(4,128)S(1)} collective-permute-done((f32[4,1024]{1,0:T(4,128)S(1)}, f32[4,1024]{1,0:T(4,128)S(1)}, u32[]{:S(2)}, u32[]{:S(2)}) %collective-permute-start.9) | collective-permute-done | bytes 16416 | tf_op jit(solution)/shard_map/ppermute | solution.py:111
  49.2 11.8 %post.4 = (bf16[2,4,1024,256]{3,2,1,0:T(8,128)(2,1)S(1)}, bf16[2,4,1024,256]{3,2,1,0:T(8,128)(2,1)S(1)}, f32[2,4,48,128]{3,2,1,0:T(8,128)S(1)}, f32[4,512]{1,0:T...) custom-call(f32[2,4,256,1024]{3,2,1,0:T(8,128)S(1)} %get-tuple-elemen, ...), custom_call_target="tpu_custom_call" | custom-call | tf_op jit(solution)/shard_map/post/pallas_call | solution.py:570
  61.0 0.8 collective-permute-start.10
  61.7 3.5 %collective-permute-start.11 = (f32[4,512]{1,0:T(4,128)S(1)}, f32[4,512]{1,0:T(4,128)S(1)}, u32[]{:S(2)}, u32[]{:S(2)}) collective-permute-start(f32[4,512]{1,0:T(4,128)S(1)} %get-tuple-element.135), channel_id=1, source_target_pairs={{0,16},{8,24},{16,0},{24,8},{1,17},{9,25},{17,1},{25,9},{2,18},{10... | collective-permute-start | bytes 24584 | tf_op jit(solution)/shard_map/ppermute | solution.py:111
  65.4 9.7 %local.5 = (f32[2,4,256,1024]{3,2,1,0:T(8,128)S(1)}, f32[2,32,1024]{2,1,0:T(8,128)S(1)}) custom-call(bf16[2,4,1024,256]{3,2,1,0:T(8,128)(2,1)S(1)} %get-tuple-element.128.t_hi.refs_20_, bf16[2,4,1024,256]{3,2,1,0:T(8,128)(2,1)S(1)} %get-tuple-element.129.t_lo.refs_21_, f32[2,4,48,128]{3,2,1,0:T(8,128)S(1)} %get-tuple-element.130.y_state, ...), custom_call_target="tpu_custom_call" | custom-call | tf_op jit(solution)/shard_map/local/pallas_call | solution.py:518
  75.1 2.3 %link.5 = (f32[2,4,8,1024]{3,2,1,0:T(8,128)S(1)}, f32[2,8,1024]{2,1,0:T(8,128)S(1)}, f32[4,1024]{1,0:T(4,128)S(1)}, f32[4,1024]{1,0:T(4,128)S(1)}, f32[4,1024]{1...) custom-call(f32[2,32,1024]{2,1,0:T(8,128)S(1)} %get-tuple-element.13, ...), custom_call_target="tpu_custom_call" | custom-call | tf_op jit(solution)/shard_map/link/pallas_call | solution.py:520
  77.5 0.6 collective-permute-start.14
  78.1 1.3 collective-permute-start.15
  79.9 1.2 collective-permute-start.17
  81.1 0.6 collective-permute-start.18
  81.7 2.1 %collective-permute-start.19 = (f32[4,1024]{1,0:T(4,128)S(1)}, f32[4,1024]{1,0:T(4,128)S(1)}, u32[]{:S(2)}, u32[]{:S(2)}) collective-permute-start(f32[4,1024]{1,0:T(4,128)S(1)} %get-tuple-element.146), channel_id=1, source_target_pairs={{0,7},{1,6},{2,5},{3,4},{4,3},{5,2},{6,1},{7,0},{8,15},{9,14},{10,... | collective-permute-start | bytes 49160 | tf_op jit(solution)/shard_map/ppermute | solution.py:111
  83.8 2.1 %collective-permute-done.18.refs_14_ = f32[4,1024]{1,0:T(4,128)S(1)} collective-permute-done((f32[4,1024]{1,0:T(4,128)S(1)}, f32[4,1024]{1,0:T(4,128)S(1)}, u32[]{:S(2)}, u32[]{:S(2)}) %collective-permute-start.18) | collective-permute-done | bytes 16416 | tf_op jit(solution)/shard_map/ppermute | solution.py:111
  85.9 12.3 %post.5 = (bf16[2,4,1024,256]{3,2,1,0:T(8,128)(2,1)S(1)}, bf16[2,4,1024,256]{3,2,1,0:T(8,128)(2,1)S(1)}, f32[2,4,48,128]{3,2,1,0:T(8,128)S(1)}, f32[4,512]{1,0:T...) custom-call(f32[2,4,256,1024]{3,2,1,0:T(8,128)S(1)} %get-tuple-elemen, ...), custom_call_target="tpu_custom_call" | custom-call | tf_op jit(solution)/shard_map/post/pallas_call | solution.py:570
  98.6 3.8 %collective-permute-start.21 = (f32[4,512]{1,0:T(4,128)S(1)}, f32[4,512]{1,0:T(4,128)S(1)}, u32[]{:S(2)}, u32[]{:S(2)}) collective-permute-start(f32[4,512]{1,0:T(4,128)S(1)} %get-tuple-element.154), channel_id=1, source_target_pairs={{0,16},{8,24},{16,0},{24,8},{1,17},{9,25},{17,1},{25,9},{2,18},{10... | collective-permute-start | bytes 24584 | tf_op jit(solution)/shard_map/ppermute | solution.py:111
  102.6 9.7 %local.6 = (f32[2,4,256,1024]{3,2,1,0:T(8,128)S(1)}, f32[2,32,1024]{2,1,0:T(8,128)S(1)}) custom-call(bf16[2,4,1024,256]{3,2,1,0:T(8,128)(2,1)S(1)} %get-tuple-element.147.t_hi, bf16[2,4,1024,256]{3,2,1,0:T(8,128)(2,1)S(1)} %get-tuple-element.148.t_lo, f32[2,4,48,128]{3,2,1,0:T(8,128)S(1)} %get-tuple-element.149.y_state, ...), custom_call_target="tpu_custom_call" | custom-call | tf_op jit(solution)/shard_map/local/pallas_call | solution.py:518
  112.3 2.3 %link.6 = (f32[2,4,8,1024]{3,2,1,0:T(8,128)S(1)}, f32[2,8,1024]{2,1,0:T(8,128)S(1)}, f32[4,1024]{1,0:T(4,128)S(1)}, f32[4,1024]{1,0:T(4,128)S(1)}, f32[4,1024]{1...) custom-call(f32[2,32,1024]{2,1,0:T(8,128)S(1)} %get-tuple-element.15, ...), custom_call_target="tpu_custom_call" | custom-call | tf_op jit(solution)/shard_map/link/pallas_call | solution.py:520
  114.7 1.3 collective-permute-start.24
  116.0 0.6 collective-permute-start.25
  116.6 1.3 collective-permute-start.26
  118.3 2.2 %collective-permute-start.28 = (f32[4,1024]{1,0:T(4,128)S(1)}, f32[4,1024]{1,0:T(4,128)S(1)}, u32[]{:S(2)}, u32[]{:S(2)}) collective-permute-start(f32[4,1024]{1,0:T(4,128)S(1)} %get-tuple-element.164), channel_id=1, source_target_pairs={{0,6},{1,7},{2,4},{3,5},{4,2},{5,3},{6,0},{7,1},{8,14},{9,15},{10,... | collective-permute-start | bytes 49160 | tf_op jit(solution)/shard_map/ppermute | solution.py:111
  121.0 1.9 %collective-permute-done.28.refs_14_ = f32[4,1024]{1,0:T(4,128)S(1)} collective-permute-done((f32[4,1024]{1,0:T(4,128)S(1)}, f32[4,1024]{1,0:T(4,128)S(1)}, u32[]{:S(2)}, u32[]{:S(2)}) %collective-permute-start.28) | collective-permute-done | bytes 16416 | tf_op jit(solution)/shard_map/ppermute | solution.py:111
  122.9 1.6 collective-permute-done.29.refs_15_
  124.5 13.6 %post.6 = (bf16[2,4,1024,256]{3,2,1,0:T(8,128)(2,1)S(1)}, bf16[2,4,1024,256]{3,2,1,0:T(8,128)(2,1)S(1)}, f32[2,4,48,128]{3,2,1,0:T(8,128)S(1)}, f32[4,512]{1,0:T...) custom-call(f32[2,4,256,1024]{3,2,1,0:T(8,128)S(1)} %get-tuple-eleme, ...), custom_call_target="tpu_custom_call", output_to_operand_aliasing={{7}: (23, {})} | custom-call | tf_op jit(solution)/shard_map/post/pallas_call | solution.py:570
  138.6 3.8 %collective-permute-start.31 = (f32[4,512]{1,0:T(4,128)S(1)}, f32[4,512]{1,0:T(4,128)S(1)}, u32[]{:S(2)}, u32[]{:S(2)}) collective-permute-start(f32[4,512]{1,0:T(4,128)S(1)} %get-tuple-element.175), channel_id=1, source_target_pairs={{0,16},{8,24},{16,0},{24,8},{1,17},{9,25},{17,1},{25,9},{2,18},{10... | collective-permute-start | bytes 24584 | tf_op jit(solution)/shard_map/ppermute | solution.py:111
  142.6 9.7 %local.7 = (f32[2,4,256,1024]{3,2,1,0:T(8,128)S(1)}, f32[2,32,1024]{2,1,0:T(8,128)S(1)}) custom-call(bf16[2,4,1024,256]{3,2,1,0:T(8,128)(2,1)S(1)} %get-tuple-element.168.t_hi, bf16[2,4,1024,256]{3,2,1,0:T(8,128)(2,1)S(1)} %get-tuple-element.169.t_lo, f32[2,4,48,128]{3,2,1,0:T(8,128)S(1)} %get-tuple-element.170.y_state, ...), custom_call_target="tpu_custom_call" | custom-call | tf_op jit(solution)/shard_map/local/pallas_call | solution.py:518
  152.3 2.3 %link.7 = (f32[2,4,8,1024]{3,2,1,0:T(8,128)S(1)}, f32[2,8,1024]{2,1,0:T(8,128)S(1)}, f32[4,1024]{1,0:T(4,128)S(1)}, f32[4,1024]{1,0:T(4,128)S(1)}, f32[4,1024]{1...) custom-call(f32[2,32,1024]{2,1,0:T(8,128)S(1)} %get-tuple-element.17, ...), custom_call_target="tpu_custom_call" | custom-call | tf_op jit(solution)/shard_map/link/pallas_call | solution.py:520
  154.7 0.6 collective-permute-start.34
  155.3 1.3 collective-permute-start.35
  157.1 1.2 collective-permute-start.37
  158.2 0.8 collective-permute-start.38
  159.0 1.9 %collective-permute-start.39 = (f32[4,1024]{1,0:T(4,128)S(1)}, f32[4,1024]{1,0:T(4,128)S(1)}, u32[]{:S(2)}, u32[]{:S(2)}) collective-permute-start(f32[4,1024]{1,0:T(4,128)S(1)} %get-tuple-element.186), channel_id=1, source_target_pairs={{0,7},{1,6},{2,5},{3,4},{4,3},{5,2},{6,1},{7,0},{8,15},{9,14},{10,... | collective-permute-start | bytes 49160 | tf_op jit(solution)/shard_map/ppermute | solution.py:111
  161.0 1.9 %collective-permute-done.38.refs_14_ = f32[4,1024]{1,0:T(4,128)S(1)} collective-permute-done((f32[4,1024]{1,0:T(4,128)S(1)}, f32[4,1024]{1,0:T(4,128)S(1)}, u32[]{:S(2)}, u32[]{:S(2)}) %collective-permute-start.38) | collective-permute-done | bytes 16416 | tf_op jit(solution)/shard_map/ppermute | solution.py:111
  163.1 9.0 %post.7 = (f32[2,1,512,1024]{3,2,1,0:T(8,128)}, f32[2,1,512,1024]{3,2,1,0:T(8,128)}, f32[4,512,1024]{2,1,0:T(8,128)}) custom-call(f32[2,4,256,1024]{3,2,1,0:T(8,128)S(1)} %get-tuple-element.171.refs_0_, f32[2,4,8,1024]{3,2,1,0:T(8,128)S(1)} %get-tuple-element.177.refs_1_, ...), custom_call_target="tpu_custom_call", output_to_operand_aliasing={{2}: (18, {})} | custom-call | tf_op jit(solution)/shard_map/post/pallas_call | solution.py:570
  (151 shorter events, 9.4 us)
Async XLA Ops:
  0.7 7.9 %copy-start.9 = (f32[512]{0:T(512)S(1)}, f32[512]{0:T(512)}, u32[]{:S(2)}) copy-start(f32[512]{0:T(512)} %constant.64) | copy-start | bytes 6148
  0.7 8.1 %copy-start.7 = (f32[1024]{0:T(1024)S(1)}, f32[1024]{0:T(1024)}, u32[]{:S(2)}) copy-start(f32[1024]{0:T(1024)} %constant.62) | copy-start | bytes 12292
  0.7 8.1 %copy-start.8 = (f32[1024]{0:T(1024)S(1)}, f32[1024]{0:T(1024)}, u32[]{:S(2)}) copy-start(f32[1024]{0:T(1024)} %constant.61) | copy-start | bytes 12292
  0.7 8.3 %copy-start.4 = (f32[10,512]{1,0:T(8,128)S(1)}, f32[10,512]{1,0:T(8,128)}, u32[]{:S(2)}) copy-start(f32[10,512]{1,0:T(8,128)} %constant.60) | copy-start | bytes 61444
  0.7 8.3 %copy-start.6 = (pred[10,512]{1,0:T(8,128)(4,1)S(1)}, pred[10,512]{1,0:T(8,128)(4,1)}, u32[]{:S(2)}) copy-start(pred[10,512]{1,0:T(8,128)(4,1)} %constant.54.clone) | copy-start | bytes 15364
  21.1 15.3 %collective-permute-start = (f32[4,512]{1,0:T(4,128)S(1)}, f32[4,512]{1,0:T(4,128)S(1)}, u32[]{:S(2)}, u32[]{:S(2)}) collective-permute-start(f32[4,512]{1,0:T(4,128)S(1)} %get-tuple-element.113), channel_id=1, source_target_pairs={{0,8},{8,0},{16,24},{24,16},{1,9},{9,1},{17,25},{25,17},{2,10},{10... | collective-permute-start | bytes 24584 | tf_op jit(solution)/shard_map/ppermute | solution.py:111
  24.2 12.3 %collective-permute-start.1 = (f32[4,512]{1,0:T(4,128)S(1)}, f32[4,512]{1,0:T(4,128)S(1)}, u32[]{:S(2)}, u32[]{:S(2)}) collective-permute-start(f32[4,512]{1,0:T(4,128)S(1)} %get-tuple-element.114), channel_id=1, source_target_pairs={{0,16},{8,24},{16,0},{24,8},{1,17},{9,25},{17,1},{25,9},{2,18},{10... | collective-permute-start | bytes 24584 | tf_op jit(solution)/shard_map/ppermute | solution.py:111
  26.8 9.7 %collective-permute-start.2 = (f32[4,512]{1,0:T(4,128)S(1)}, f32[4,512]{1,0:T(4,128)S(1)}, u32[]{:S(2)}, u32[]{:S(2)}) collective-permute-start(f32[4,512]{1,0:T(4,128)S(1)} %get-tuple-element.115), channel_id=1, source_target_pairs={{0,24},{8,16},{16,8},{24,0},{1,25},{9,17},{17,9},{25,1},{2,26},{10... | collective-permute-start | bytes 24584 | tf_op jit(solution)/shard_map/ppermute | solution.py:111
  26.8 9.7 %copy-start.2 = (f32[32,1024]{1,0:T(8,128)S(1)}, f32[32,1024]{1,0:T(8,128)}, u32[]{:S(2)}) copy-start(f32[32,1024]{1,0:T(8,128)} %get-tuple-element.109.sx) | copy-start | bytes 393220
  38.8 3.7 %collective-permute-start.3 = (f32[4,1024]{1,0:T(4,128)S(1)}, f32[4,1024]{1,0:T(4,128)S(1)}, u32[]{:S(2)}, u32[]{:S(2)}) collective-permute-start(f32[4,1024]{1,0:T(4,128)S(1)} %get-tuple-element.121), channel_id=1, source_target_pairs={{0,1},{1,0},{2,3},{3,2},{4,5},{5,4},{6,7},{7,6},{8,9},{9,8},{10,11... | collective-permute-start | bytes 49160 | tf_op jit(solution)/shard_map/ppermute | solution.py:111
  38.9 6.2 %collective-permute-start.4 = (f32[4,1024]{1,0:T(4,128)S(1)}, f32[4,1024]{1,0:T(4,128)S(1)}, u32[]{:S(2)}, u32[]{:S(2)}) collective-permute-start(f32[4,1024]{1,0:T(4,128)S(1)} %get-tuple-element.122), channel_id=1, source_target_pairs={{0,2},{1,3},{2,0},{3,1},{4,6},{5,7},{6,4},{7,5},{8,10},{9,11},{10,... | collective-permute-start | bytes 49160 | tf_op jit(solution)/shard_map/ppermute | solution.py:111
  40.7 4.6 %collective-permute-start.5 = (f32[4,1024]{1,0:T(4,128)S(1)}, f32[4,1024]{1,0:T(4,128)S(1)}, u32[]{:S(2)}, u32[]{:S(2)}) collective-permute-start(f32[4,1024]{1,0:T(4,128)S(1)} %get-tuple-element.123), channel_id=1, source_target_pairs={{0,3},{1,2},{2,1},{3,0},{4,7},{5,6},{6,5},{7,4},{8,11},{9,10},{10,... | collective-permute-start | bytes 49160 | tf_op jit(solution)/shard_map/ppermute | solution.py:111
  40.8 4.5 %collective-permute-start.6 = (f32[4,1024]{1,0:T(4,128)S(1)}, f32[4,1024]{1,0:T(4,128)S(1)}, u32[]{:S(2)}, u32[]{:S(2)}) collective-permute-start(f32[4,1024]{1,0:T(4,128)S(1)} %get-tuple-element.124), channel_id=1, source_target_pairs={{0,4},{1,5},{2,6},{3,7},{4,0},{5,1},{6,2},{7,3},{8,12},{9,13},{10,... | collective-permute-start | bytes 49160 | tf_op jit(solution)/shard_map/ppermute | solution.py:111
  42.5 3.2 %collective-permute-start.7 = (f32[4,1024]{1,0:T(4,128)S(1)}, f32[4,1024]{1,0:T(4,128)S(1)}, u32[]{:S(2)}, u32[]{:S(2)}) collective-permute-start(f32[4,1024]{1,0:T(4,128)S(1)} %get-tuple-element.125), channel_id=1, source_target_pairs={{0,5},{1,4},{2,7},{3,6},{4,1},{5,0},{6,3},{7,2},{8,13},{9,12},{10,... | collective-permute-start | bytes 49160 | tf_op jit(solution)/shard_map/ppermute | solution.py:111
  42.5 4.7 %collective-permute-start.8 = (f32[4,1024]{1,0:T(4,128)S(1)}, f32[4,1024]{1,0:T(4,128)S(1)}, u32[]{:S(2)}, u32[]{:S(2)}) collective-permute-start(f32[4,1024]{1,0:T(4,128)S(1)} %get-tuple-element.126), channel_id=1, source_target_pairs={{0,6},{1,7},{2,4},{3,5},{4,2},{5,3},{6,0},{7,1},{8,14},{9,15},{10,... | collective-permute-start | bytes 49160 | tf_op jit(solution)/shard_map/ppermute | solution.py:111
  45.1 4.1 %collective-permute-start.9 = (f32[4,1024]{1,0:T(4,128)S(1)}, f32[4,1024]{1,0:T(4,128)S(1)}, u32[]{:S(2)}, u32[]{:S(2)}) collective-permute-start(f32[4,1024]{1,0:T(4,128)S(1)} %get-tuple-element.127), channel_id=1, source_target_pairs={{0,7},{1,6},{2,5},{3,4},{4,3},{5,2},{6,1},{7,0},{8,15},{9,14},{10,... | collective-permute-start | bytes 49160 | tf_op jit(solution)/shard_map/ppermute | solution.py:111
  61.0 14.1 %copy-start = (bf16[2,4,1024,256]{3,2,1,0:T(8,128)(2,1)}, bf16[2,4,1024,256]{3,2,1,0:T(8,128)(2,1)S(1)}, u32[]{:S(2)}) copy-start(bf16[2,4,1024,256]{3,2,1,0:T(8,128)(2,1)S(1)} %get-tuple-element.128.t_hi.refs_20_) | copy-start | bytes 12582916
  61.0 14.1 %copy-start.1 = (bf16[2,4,1024,256]{3,2,1,0:T(8,128)(2,1)}, bf16[2,4,1024,256]{3,2,1,0:T(8,128)(2,1)S(1)}, u32[]{:S(2)}) copy-start(bf16[2,4,1024,256]{3,2,1,0:T(8,128)(2,1)S(1)} %get-tuple-element.129.t_lo.refs_21_) | copy-start | bytes 12582916
  61.0 14.1 %collective-permute-start.10 = (f32[4,512]{1,0:T(4,128)S(1)}, f32[4,512]{1,0:T(4,128)S(1)}, u32[]{:S(2)}, u32[]{:S(2)}) collective-permute-start(f32[4,512]{1,0:T(4,128)S(1)} %get-tuple-element.134), channel_id=1, source_target_pairs={{0,8},{8,0},{16,24},{24,16},{1,9},{9,1},{17,25},{25,17},{2,10},{10... | collective-permute-start | bytes 24584 | tf_op jit(solution)/shard_map/ppermute | solution.py:111
  61.7 13.4 %collective-permute-start.11 = (f32[4,512]{1,0:T(4,128)S(1)}, f32[4,512]{1,0:T(4,128)S(1)}, u32[]{:S(2)}, u32[]{:S(2)}) collective-permute-start(f32[4,512]{1,0:T(4,128)S(1)} %get-tuple-element.135), channel_id=1, source_target_pairs={{0,16},{8,24},{16,0},{24,8},{1,17},{9,25},{17,1},{25,9},{2,18},{10... | collective-permute-start | bytes 24584 | tf_op jit(solution)/shard_map/ppermute | solution.py:111
  65.2 9.9 %collective-permute-start.12 = (f32[4,512]{1,0:T(4,128)S(1)}, f32[4,512]{1,0:T(4,128)S(1)}, u32[]{:S(2)}, u32[]{:S(2)}) collective-permute-start(f32[4,512]{1,0:T(4,128)S(1)} %get-tuple-element.136), channel_id=1, source_target_pairs={{0,24},{8,16},{16,8},{24,0},{1,25},{9,17},{17,9},{25,1},{2,26},{10... | collective-permute-start | bytes 24584 | tf_op jit(solution)/shard_map/ppermute | solution.py:111
  77.4 3.6 %collective-permute-start.13 = (f32[4,1024]{1,0:T(4,128)S(1)}, f32[4,1024]{1,0:T(4,128)S(1)}, u32[]{:S(2)}, u32[]{:S(2)}) collective-permute-start(f32[4,1024]{1,0:T(4,128)S(1)} %get-tuple-element.140), channel_id=1, source_target_pairs={{0,1},{1,0},{2,3},{3,2},{4,5},{5,4},{6,7},{7,6},{8,9},{9,8},{10,11... | collective-permute-start | bytes 49160 | tf_op jit(solution)/shard_map/ppermute | solution.py:111
  77.5 4.2 %collective-permute-start.14 = (f32[4,1024]{1,0:T(4,128)S(1)}, f32[4,1024]{1,0:T(4,128)S(1)}, u32[]{:S(2)}, u32[]{:S(2)}) collective-permute-start(f32[4,1024]{1,0:T(4,128)S(1)} %get-tuple-element.141), channel_id=1, source_target_pairs={{0,2},{1,3},{2,0},{3,1},{4,6},{5,7},{6,4},{7,5},{8,10},{9,11},{10,... | collective-permute-start | bytes 49160 | tf_op jit(solution)/shard_map/ppermute | solution.py:111
  78.1 5.7 %collective-permute-start.15 = (f32[4,1024]{1,0:T(4,128)S(1)}, f32[4,1024]{1,0:T(4,128)S(1)}, u32[]{:S(2)}, u32[]{:S(2)}) collective-permute-start(f32[4,1024]{1,0:T(4,128)S(1)} %get-tuple-element.142), channel_id=1, source_target_pairs={{0,3},{1,2},{2,1},{3,0},{4,7},{5,6},{6,5},{7,4},{8,11},{9,10},{10,... | collective-permute-start | bytes 49160 | tf_op jit(solution)/shard_map/ppermute | solution.py:111
  79.4 4.4 %collective-permute-start.16 = (f32[4,1024]{1,0:T(4,128)S(1)}, f32[4,1024]{1,0:T(4,128)S(1)}, u32[]{:S(2)}, u32[]{:S(2)}) collective-permute-start(f32[4,1024]{1,0:T(4,128)S(1)} %get-tuple-element.143), channel_id=1, source_target_pairs={{0,4},{1,5},{2,6},{3,7},{4,0},{5,1},{6,2},{7,3},{8,12},{9,13},{10,... | collective-permute-start | bytes 49160 | tf_op jit(solution)/shard_map/ppermute | solution.py:111
  79.9 3.9 %collective-permute-start.17 = (f32[4,1024]{1,0:T(4,128)S(1)}, f32[4,1024]{1,0:T(4,128)S(1)}, u32[]{:S(2)}, u32[]{:S(2)}) collective-permute-start(f32[4,1024]{1,0:T(4,128)S(1)} %get-tuple-element.144), channel_id=1, source_target_pairs={{0,5},{1,4},{2,7},{3,6},{4,1},{5,0},{6,3},{7,2},{8,13},{9,12},{10,... | collective-permute-start | bytes 49160 | tf_op jit(solution)/shard_map/ppermute | solution.py:111
  81.1 4.8 %collective-permute-start.18 = (f32[4,1024]{1,0:T(4,128)S(1)}, f32[4,1024]{1,0:T(4,128)S(1)}, u32[]{:S(2)}, u32[]{:S(2)}) collective-permute-start(f32[4,1024]{1,0:T(4,128)S(1)} %get-tuple-element.145), channel_id=1, source_target_pairs={{0,6},{1,7},{2,4},{3,5},{4,2},{5,3},{6,0},{7,1},{8,14},{9,15},{10,... | collective-permute-start | bytes 49160 | tf_op jit(solution)/shard_map/ppermute | solution.py:111
  81.7 4.2 %collective-permute-start.19 = (f32[4,1024]{1,0:T(4,128)S(1)}, f32[4,1024]{1,0:T(4,128)S(1)}, u32[]{:S(2)}, u32[]{:S(2)}) collective-permute-start(f32[4,1024]{1,0:T(4,128)S(1)} %get-tuple-element.146), channel_id=1, source_target_pairs={{0,7},{1,6},{2,5},{3,4},{4,3},{5,2},{6,1},{7,0},{8,15},{9,14},{10,... | collective-permute-start | bytes 49160 | tf_op jit(solution)/shard_map/ppermute | solution.py:111
  98.2 14.1 %collective-permute-start.20 = (f32[4,512]{1,0:T(4,128)S(1)}, f32[4,512]{1,0:T(4,128)S(1)}, u32[]{:S(2)}, u32[]{:S(2)}) collective-permute-start(f32[4,512]{1,0:T(4,128)S(1)} %get-tuple-element.153), channel_id=1, source_target_pairs={{0,8},{8,0},{16,24},{24,16},{1,9},{9,1},{17,25},{25,17},{2,10},{10... | collective-permute-start | bytes 24584 | tf_op jit(solution)/shard_map/ppermute | solution.py:111
  98.6 13.7 %collective-permute-start.21 = (f32[4,512]{1,0:T(4,128)S(1)}, f32[4,512]{1,0:T(4,128)S(1)}, u32[]{:S(2)}, u32[]{:S(2)}) collective-permute-start(f32[4,512]{1,0:T(4,128)S(1)} %get-tuple-element.154), channel_id=1, source_target_pairs={{0,16},{8,24},{16,0},{24,8},{1,17},{9,25},{17,1},{25,9},{2,18},{10... | collective-permute-start | bytes 24584 | tf_op jit(solution)/shard_map/ppermute | solution.py:111
  102.4 9.9 %collective-permute-start.22 = (f32[4,512]{1,0:T(4,128)S(1)}, f32[4,512]{1,0:T(4,128)S(1)}, u32[]{:S(2)}, u32[]{:S(2)}) collective-permute-start(f32[4,512]{1,0:T(4,128)S(1)} %get-tuple-element.155), channel_id=1, source_target_pairs={{0,24},{8,16},{16,8},{24,0},{1,25},{9,17},{17,9},{25,1},{2,26},{10... | collective-permute-start | bytes 24584 | tf_op jit(solution)/shard_map/ppermute | solution.py:111
  114.6 3.6 %collective-permute-start.23 = (f32[4,1024]{1,0:T(4,128)S(1)}, f32[4,1024]{1,0:T(4,128)S(1)}, u32[]{:S(2)}, u32[]{:S(2)}) collective-permute-start(f32[4,1024]{1,0:T(4,128)S(1)} %get-tuple-element.159), channel_id=1, source_target_pairs={{0,1},{1,0},{2,3},{3,2},{4,5},{5,4},{6,7},{7,6},{8,9},{9,8},{10,11... | collective-permute-start | bytes 49160 | tf_op jit(solution)/shard_map/ppermute | solution.py:111
  114.7 5.7 %collective-permute-start.24 = (f32[4,1024]{1,0:T(4,128)S(1)}, f32[4,1024]{1,0:T(4,128)S(1)}, u32[]{:S(2)}, u32[]{:S(2)}) collective-permute-start(f32[4,1024]{1,0:T(4,128)S(1)} %get-tuple-element.160), channel_id=1, source_target_pairs={{0,2},{1,3},{2,0},{3,1},{4,6},{5,7},{6,4},{7,5},{8,10},{9,11},{10,... | collective-permute-start | bytes 49160 | tf_op jit(solution)/shard_map/ppermute | solution.py:111
  116.0 5.0 %collective-permute-start.25 = (f32[4,1024]{1,0:T(4,128)S(1)}, f32[4,1024]{1,0:T(4,128)S(1)}, u32[]{:S(2)}, u32[]{:S(2)}) collective-permute-start(f32[4,1024]{1,0:T(4,128)S(1)} %get-tuple-element.161), channel_id=1, source_target_pairs={{0,3},{1,2},{2,1},{3,0},{4,7},{5,6},{6,5},{7,4},{8,11},{9,10},{10,... | collective-permute-start | bytes 49160 | tf_op jit(solution)/shard_map/ppermute | solution.py:111
  116.6 4.4 %collective-permute-start.26 = (f32[4,1024]{1,0:T(4,128)S(1)}, f32[4,1024]{1,0:T(4,128)S(1)}, u32[]{:S(2)}, u32[]{:S(2)}) collective-permute-start(f32[4,1024]{1,0:T(4,128)S(1)} %get-tuple-element.162), channel_id=1, source_target_pairs={{0,4},{1,5},{2,6},{3,7},{4,0},{5,1},{6,2},{7,3},{8,12},{9,13},{10,... | collective-permute-start | bytes 49160 | tf_op jit(solution)/shard_map/ppermute | solution.py:111
  117.8 3.2 %collective-permute-start.27 = (f32[4,1024]{1,0:T(4,128)S(1)}, f32[4,1024]{1,0:T(4,128)S(1)}, u32[]{:S(2)}, u32[]{:S(2)}) collective-permute-start(f32[4,1024]{1,0:T(4,128)S(1)} %get-tuple-element.163), channel_id=1, source_target_pairs={{0,5},{1,4},{2,7},{3,6},{4,1},{5,0},{6,3},{7,2},{8,13},{9,12},{10,... | collective-permute-start | bytes 49160 | tf_op jit(solution)/shard_map/ppermute | solution.py:111
  118.3 4.6 %collective-permute-start.28 = (f32[4,1024]{1,0:T(4,128)S(1)}, f32[4,1024]{1,0:T(4,128)S(1)}, u32[]{:S(2)}, u32[]{:S(2)}) collective-permute-start(f32[4,1024]{1,0:T(4,128)S(1)} %get-tuple-element.164), channel_id=1, source_target_pairs={{0,6},{1,7},{2,4},{3,5},{4,2},{5,3},{6,0},{7,1},{8,14},{9,15},{10,... | collective-permute-start | bytes 49160 | tf_op jit(solution)/shard_map/ppermute | solution.py:111
  120.4 4.1 %collective-permute-start.29 = (f32[4,1024]{1,0:T(4,128)S(1)}, f32[4,1024]{1,0:T(4,128)S(1)}, u32[]{:S(2)}, u32[]{:S(2)}) collective-permute-start(f32[4,1024]{1,0:T(4,128)S(1)} %get-tuple-element.165), channel_id=1, source_target_pairs={{0,7},{1,6},{2,5},{3,4},{4,3},{5,2},{6,1},{7,0},{8,15},{9,14},{10,... | collective-permute-start | bytes 49160 | tf_op jit(solution)/shard_map/ppermute | solution.py:111
  138.2 14.1 %collective-permute-start.30 = (f32[4,512]{1,0:T(4,128)S(1)}, f32[4,512]{1,0:T(4,128)S(1)}, u32[]{:S(2)}, u32[]{:S(2)}) collective-permute-start(f32[4,512]{1,0:T(4,128)S(1)} %get-tuple-element.174), channel_id=1, source_target_pairs={{0,8},{8,0},{16,24},{24,16},{1,9},{9,1},{17,25},{25,17},{2,10},{10... | collective-permute-start | bytes 24584 | tf_op jit(solution)/shard_map/ppermute | solution.py:111
  138.6 13.7 %collective-permute-start.31 = (f32[4,512]{1,0:T(4,128)S(1)}, f32[4,512]{1,0:T(4,128)S(1)}, u32[]{:S(2)}, u32[]{:S(2)}) collective-permute-start(f32[4,512]{1,0:T(4,128)S(1)} %get-tuple-element.175), channel_id=1, source_target_pairs={{0,16},{8,24},{16,0},{24,8},{1,17},{9,25},{17,1},{25,9},{2,18},{10... | collective-permute-start | bytes 24584 | tf_op jit(solution)/shard_map/ppermute | solution.py:111
  142.4 9.9 %collective-permute-start.32 = (f32[4,512]{1,0:T(4,128)S(1)}, f32[4,512]{1,0:T(4,128)S(1)}, u32[]{:S(2)}, u32[]{:S(2)}) collective-permute-start(f32[4,512]{1,0:T(4,128)S(1)} %get-tuple-element.176), channel_id=1, source_target_pairs={{0,24},{8,16},{16,8},{24,0},{1,25},{9,17},{17,9},{25,1},{2,26},{10... | collective-permute-start | bytes 24584 | tf_op jit(solution)/shard_map/ppermute | solution.py:111
  154.6 3.6 %collective-permute-start.33 = (f32[4,1024]{1,0:T(4,128)S(1)}, f32[4,1024]{1,0:T(4,128)S(1)}, u32[]{:S(2)}, u32[]{:S(2)}) collective-permute-start(f32[4,1024]{1,0:T(4,128)S(1)} %get-tuple-element.180), channel_id=1, source_target_pairs={{0,1},{1,0},{2,3},{3,2},{4,5},{5,4},{6,7},{7,6},{8,9},{9,8},{10,11... | collective-permute-start | bytes 49160 | tf_op jit(solution)/shard_map/ppermute | solution.py:111
  154.7 4.3 %collective-permute-start.34 = (f32[4,1024]{1,0:T(4,128)S(1)}, f32[4,1024]{1,0:T(4,128)S(1)}, u32[]{:S(2)}, u32[]{:S(2)}) collective-permute-start(f32[4,1024]{1,0:T(4,128)S(1)} %get-tuple-element.181), channel_id=1, source_target_pairs={{0,2},{1,3},{2,0},{3,1},{4,6},{5,7},{6,4},{7,5},{8,10},{9,11},{10,... | collective-permute-start | bytes 49160 | tf_op jit(solution)/shard_map/ppermute | solution.py:111
  155.3 5.7 %collective-permute-start.35 = (f32[4,1024]{1,0:T(4,128)S(1)}, f32[4,1024]{1,0:T(4,128)S(1)}, u32[]{:S(2)}, u32[]{:S(2)}) collective-permute-start(f32[4,1024]{1,0:T(4,128)S(1)} %get-tuple-element.182), channel_id=1, source_target_pairs={{0,3},{1,2},{2,1},{3,0},{4,7},{5,6},{6,5},{7,4},{8,11},{9,10},{10,... | collective-permute-start | bytes 49160 | tf_op jit(solution)/shard_map/ppermute | solution.py:111
  156.5 4.4 %collective-permute-start.36 = (f32[4,1024]{1,0:T(4,128)S(1)}, f32[4,1024]{1,0:T(4,128)S(1)}, u32[]{:S(2)}, u32[]{:S(2)}) collective-permute-start(f32[4,1024]{1,0:T(4,128)S(1)} %get-tuple-element.183), channel_id=1, source_target_pairs={{0,4},{1,5},{2,6},{3,7},{4,0},{5,1},{6,2},{7,3},{8,12},{9,13},{10,... | collective-permute-start | bytes 49160 | tf_op jit(solution)/shard_map/ppermute | solution.py:111
  157.1 3.9 %collective-permute-start.37 = (f32[4,1024]{1,0:T(4,128)S(1)}, f32[4,1024]{1,0:T(4,128)S(1)}, u32[]{:S(2)}, u32[]{:S(2)}) collective-permute-start(f32[4,1024]{1,0:T(4,128)S(1)} %get-tuple-element.184), channel_id=1, source_target_pairs={{0,5},{1,4},{2,7},{3,6},{4,1},{5,0},{6,3},{7,2},{8,13},{9,12},{10,... | collective-permute-start | bytes 49160 | tf_op jit(solution)/shard_map/ppermute | solution.py:111
  158.2 4.6 %collective-permute-start.38 = (f32[4,1024]{1,0:T(4,128)S(1)}, f32[4,1024]{1,0:T(4,128)S(1)}, u32[]{:S(2)}, u32[]{:S(2)}) collective-permute-start(f32[4,1024]{1,0:T(4,128)S(1)} %get-tuple-element.185), channel_id=1, source_target_pairs={{0,6},{1,7},{2,4},{3,5},{4,2},{5,3},{6,0},{7,1},{8,14},{9,15},{10,... | collective-permute-start | bytes 49160 | tf_op jit(solution)/shard_map/ppermute | solution.py:111
  159.0 4.1 %collective-permute-start.39 = (f32[4,1024]{1,0:T(4,128)S(1)}, f32[4,1024]{1,0:T(4,128)S(1)}, u32[]{:S(2)}, u32[]{:S(2)}) collective-permute-start(f32[4,1024]{1,0:T(4,128)S(1)} %get-tuple-element.186), channel_id=1, source_target_pairs={{0,7},{1,6},{2,5},{3,4},{4,3},{5,2},{6,1},{7,0},{8,15},{9,14},{10,... | collective-permute-start | bytes 49160 | tf_op jit(solution)/shard_map/ppermute | solution.py:111
  (4 other events, 23.9 us)
